TPU v7x, 256 devices: a whole 4x4x8 slice. The times are simulated.
256 devices in a mesh: gx: 32 (over z, x), gy: 8 (over y, core).
Axes of the slice: x: 4, y: 4, z: 8, core: 2. Of those that a mesh axis runs over, the one named last changes fastest.
Arguments:
- phase_label: int32 [512, 256, 128], P('gx', 'gy'), may hold values from 0 to 2
- tab_index: int32 [512, 256, 128], P('gx', 'gy'), may hold values from 0 to 63
- source_field: float32 [512, 256, 128], P('gx', 'gy'), may hold values from -8 to 8
- sigma_table: float32 [3], replicated, may hold values from 0.2 to 5
- pattern_gain: float32 [16, 64], replicated, may hold values from -6 to 6
Outputs:
- solution: float32 [16, 512, 256, 128], P(None, 'gx', 'gy')
- residual: float32 [16, 512, 256, 128], P(None, 'gx', 'gy')
All inputs are finite; a program needn't handle non-finite values.
Results may differ from a plain program's by a relative error of at most 0.0003.
Values sent between devices are 32-bit elements; how exact they have to be, the bound alone decides.
A program may use at most 192 MiB of HBM per device.

v0:
```python
import jax
import jax.numpy as jnp
import numpy as np
from jax import lax
from jax.sharding import PartitionSpec as P

S = 4
NRHS = 16
TABS = 64


OFFSETS = ((-1, 0, 0), (1, 0, 0), (0, -1, 0), (0, 1, 0), (0, 0, -1), (0, 0, 1))


def with_halo(value, sides, width):
    for axis, dim in sides:
        size, length = (lax.axis_size(axis), value.shape[dim])
        up = [(i, (i + 1) % size) for i in range(size - 1)]
        down = [(j, i) for i, j in up]
        last = lax.slice_in_dim(value, length - width, length, axis=dim)
        initial = lax.slice_in_dim(value, 0, width, axis=dim)
        before = lax.ppermute(last, axis, up)
        after = lax.ppermute(initial, axis, down)
        value = jnp.concatenate([before, value, after], axis=dim)
    return value


def moved(array, a, b, c):
    sx = array.shape[-3]
    sy = array.shape[-2]
    sz = array.shape[-1]
    return array[..., 1 + a : sx - 1 + a, 1 + b : sy - 1 + b, 1 + c : sz - 1 + c]


def neighbour_mean(fields, conduct):
    fields_z = jnp.pad(fields, ((0, 0), (0, 0), (0, 0), (1, 1)))
    conduct_z = jnp.pad(conduct, ((0, 0), (0, 0), (1, 1)))
    centre = moved(conduct_z, 0, 0, 0)
    summed = jnp.zeros(fields.shape[:1] + centre.shape, jnp.float32)
    weights = jnp.zeros(centre.shape, jnp.float32)
    for offset in OFFSETS:
        face = 0.5 * (centre + moved(conduct_z, offset[0], offset[1], offset[2]))
        summed = summed + face[None] * moved(fields_z, offset[0], offset[1], offset[2])
        weights = weights + face
    inside = centre > 0
    return jnp.where(inside[None], summed / jnp.where(inside, weights, 1.0)[None], 0.0)


def difference_matrix():
    matrix = np.zeros((NRHS * (S + 1), NRHS * S), np.float32)
    for step in range(S):
        for column in range(NRHS):
            matrix[step * NRHS + column, step * NRHS + column] = 1.0
            matrix[(step + 1) * NRHS + column, step * NRHS + column] = -1.0
    return jnp.asarray(matrix)


def least_squares(gram):
    highest = lax.Precision.HIGHEST
    diff = difference_matrix()
    hess = jnp.dot(diff.T, jnp.dot(gram, diff, precision=highest), precision=highest)
    right_block = jnp.dot(diff.T, gram[:, :NRHS], precision=highest)
    factor = jnp.linalg.cholesky(hess)
    coeffs = jax.scipy.linalg.cho_solve((factor, True), right_block)
    return (diff, coeffs)


def shards(phase_label, tab_index, source_field, sigma_table, pattern_gain):
    highest = lax.Precision.HIGHEST
    shape = phase_label.shape
    conduct = jnp.where(
        phase_label == 0,
        sigma_table[0],
        jnp.where(phase_label == 1, sigma_table[1], sigma_table[2]),
    )
    onehot = (tab_index.reshape(1, -1) == jnp.arange(TABS, dtype=jnp.int32)[:, None]).astype(
        jnp.float32
    )
    start = jnp.dot(pattern_gain, onehot, precision=highest) * source_field.reshape(1, -1)
    start = start.reshape((NRHS,) + shape)
    stacked = jnp.concatenate([conduct[None], start], 0)
    krylov = [start]
    ghosted = with_halo(stacked, (("gx", 1), ("gy", 2)), 1)
    conduct_wide = ghosted[0]
    current = neighbour_mean(ghosted[1:], conduct_wide)
    krylov.append(current)
    for step in range(S - 1):
        padded = with_halo(current, (("gx", 1), ("gy", 2)), 1)
        current = neighbour_mean(padded, conduct_wide)
        krylov.append(current)
    flat = jnp.concatenate([field.reshape(NRHS, -1) for field in krylov], 0)
    gram = lax.psum(jnp.dot(flat, flat.T, precision=highest), ("gx", "gy"))
    diff, coeffs = least_squares(gram)
    solution = jnp.dot(coeffs.T, flat[: S * NRHS], precision=highest)
    combined = jnp.dot(diff, coeffs, precision=highest)
    residual = flat[:NRHS] - jnp.dot(combined.T, flat, precision=highest)
    return (solution.reshape((NRHS,) + shape), residual.reshape((NRHS,) + shape))


def solution(mesh):
    placed = (P("gx", "gy", None), P("gx", "gy", None), P("gx", "gy", None), P(), P())
    return jax.shard_map(
        shards,
        mesh=mesh,
        in_specs=placed,
        out_specs=(P(None, "gx", "gy", None), P(None, "gx", "gy", None)),
        check_vma=False,
    )
```

profile of v0, /device:TPU:1, one launch (start us, length us, event | category | flops | bytes accessed | tf_op | source)
XLA Modules:
  0.0 357.0 jit_solution(16355060055221915815)
XLA Ops:
  2.1 7.5 %constant_dynamic-update-slice_fusion.3 = (f32[80,65536]{1,0:T(8,128)}, f32[65536,16]{0,1:T(8,128)S(1)}) fusion(f32[65536]{0:T(1024)} %bitcast.93, f32[16,64]{1,0:T(8,128)S(1)} %copy-done, s32[65536]{0:T(1024)} %bitcast.94), kind=kOutput, calls=%fused_computation.175 | convolution fusion | flops 810549248 | bytes 8916992 | tf_op jit(solution)/shard_map/dot_general | solution.py:79
  18.9 4.0 %collective-permute-done = f32[17,1,32,128]{3,2,1,0:T(8,128)S(1)} collective-permute-done((f32[17,1,32,128]{3,2,1,0:T(8,128)S(1)}, f32[17,1,32,128]{3,2,1,0:T(8,128)S(1)}, u32[]{:S(2)}, u32[]{:S(2)}) %collective-permute-start) | collective-permute-done | bytes 278560 | tf_op jit(solution)/shard_map/ppermute | solution.py:22
  26.9 5.0 %collective-permute-start.2 = (f32[17,18,1,128]{3,2,1,0:T(1,128)S(1)}, f32[17,18,1,128]{3,2,1,0:T(1,128)S(1)}, u32[]{:S(2)}, u32[]{:S(2)}) collective-permute-start(f32[17,18,1,128]{3,2,1,0:T(1,128)S(1)} %get-tuple-element.10), channel_id=1, source_target_pairs={{0,1},{1,2},{2,3},{3,4},{4,5},{5,6},{6,7},{8,9},{9,10},{10,11},{11... | collective-permute-start | bytes 470024 | tf_op jit(solution)/shard_map/ppermute | solution.py:22
  34.1 4.4 %collective-permute-done.3 = f32[17,18,1,128]{3,2,1,0:T(1,128)S(1)} collective-permute-done((f32[17,18,1,128]{3,2,1,0:T(1,128)S(1)}, f32[17,18,1,128]{3,2,1,0:T(1,128)S(1)}, u32[]{:S(2)}, u32[]{:S(2)}) %collective-permute-start.3) | collective-permute-done | bytes 156704 | tf_op jit(solution)/shard_map/ppermute | solution.py:23
  39.7 9.6 %select_maximum_fusion.12 = f32[16,18,34,130]{3,2,1,0:T(8,128)} fusion(f32[17,18,1,128]{3,2,1,0:T(1,128)S(1)} %collective-permute-done.3, f32[17,18,1,128]{3,2,1,0:T(1,128)S(1)} %collective-permute-done.2, f32[17,1,32,128]{3,2,1,0:T(8,128)S(1)} %collective-permute-done.1, f32[17,1,32,128]{3,2,1,0:T(8,128)S(1)} %collective-permute-done, ...), kind=kLoop, calls=%fused_computation.25 | loop fusion | flops 17821440 | bytes 10418688 | tf_op jit(solution)/shard_map/concatenate | solution.py:24
  49.3 9.0 %fusion.45 = f32[16,16,32,128]{3,2,1,0:T(8,128)S(1)} fusion(f32[16,18,34,130]{3,2,1,0:T(8,128)} %select_maximum_fusion.12, f32[17,18,1,128]{3,2,1,0:T(1,128)} %copy-done.13, f32[17,1,32,128]{3,2,1,0:T(8,128)} %copy-done.9, f32[17,1,32,128]{3,2,1,0:T(8,128)} %copy-done.8, f32[16,16,32,128]{3,2,1,0:T(8,128)S(1)} %bitcast.84, ...), kind=kLoop, calls=%fused_computation.102 | loop fusion | flops 26214400 | bytes 19810304 | tf_op jit(solution)/shard_map/jit(_where)/select_n | solution.py:46
  64.8 4.1 %collective-permute-done.5 = f32[16,1,32,128]{3,2,1,0:T(8,128)S(1)} collective-permute-done((f32[16,1,32,128]{3,2,1,0:T(8,128)S(1)}, f32[16,1,32,128]{3,2,1,0:T(8,128)S(1)}, u32[]{:S(2)}, u32[]{:S(2)}) %collective-permute-start.5) | collective-permute-done | bytes 262176 | tf_op jit(solution)/shard_map/ppermute | solution.py:23
  69.1 5.2 %collective-permute-start.6 = (f32[16,18,1,128]{3,2,1,0:T(1,128)S(1)}, f32[16,18,1,128]{3,2,1,0:T(1,128)S(1)}, u32[]{:S(2)}, u32[]{:S(2)}) collective-permute-start(f32[16,18,1,128]{3,2,1,0:T(1,128)S(1)} %get-tuple-element.16), channel_id=1, source_target_pairs={{0,1},{1,2},{2,3},{3,4},{4,5},{5,6},{6,7},{8,9},{9,10},{10,11},{11... | collective-permute-start | bytes 442376 | tf_op jit(solution)/shard_map/ppermute | solution.py:22
  76.6 4.4 %collective-permute-done.7 = f32[16,18,1,128]{3,2,1,0:T(1,128)S(1)} collective-permute-done((f32[16,18,1,128]{3,2,1,0:T(1,128)S(1)}, f32[16,18,1,128]{3,2,1,0:T(1,128)S(1)}, u32[]{:S(2)}, u32[]{:S(2)}) %collective-permute-start.7) | collective-permute-done | bytes 147488 | tf_op jit(solution)/shard_map/ppermute | solution.py:23
  80.9 8.9 %select_maximum_fusion.8 = f32[16,18,34,130]{3,2,1,0:T(8,128)} fusion(f32[16,18,1,128]{3,2,1,0:T(1,128)S(1)} %collective-permute-done.7, f32[16,18,1,128]{3,2,1,0:T(1,128)S(1)} %collective-permute-done.6, f32[16,1,32,128]{3,2,1,0:T(8,128)S(1)} %collective-permute-done.5, f32[16,16,32,128]{3,2,1,0:T(8,128)S(1)} %fusion.45, ...), kind=kLoop, calls=%fused_computation.21 | loop fusion | flops 15275520 | bytes 10105344 | tf_op jit(solution)/shard_map/concatenate | solution.py:24
  89.8 10.9 %fusion.34 = f32[16,16,32,128]{3,2,1,0:T(8,128)S(1)} fusion(f32[16,18,34,130]{3,2,1,0:T(8,128)} %select_maximum_fusion.8, f32[16,18,1,128]{3,2,1,0:T(1,128)S(1)} %collective-permute-done.7, f32[16,1,32,128]{3,2,1,0:T(8,128)S(1)} %collective-permute-done.5, f32[16,16,32,128]{3,2,1,0:T(8,128)S(1)} %fusion.45, ...), kind=kLoop, calls=%fused_computation.81 | loop fusion | flops 22020096 | bytes 19496960 | tf_op jit(solution)/shard_map/jit(_where)/select_n | solution.py:46
  100.7 4.4 %collective-permute-start.8 = (f32[16,1,32,128]{3,2,1,0:T(8,128)S(1)}, f32[16,1,32,128]{3,2,1,0:T(8,128)S(1)}, u32[]{:S(2)}, u32[]{:S(2)}) collective-permute-start(f32[16,1,32,128]{3,2,1,0:T(8,128)S(1)} %get-tuple-element.22), channel_id=1, source_target_pairs={{0,8},{8,16},{16,24},{24,32},{32,40},{40,48},{48,56},{56,64},{64,7... | collective-permute-start | bytes 786440 | tf_op jit(solution)/shard_map/ppermute | solution.py:22
  108.5 4.4 %collective-permute-done.9 = f32[16,1,32,128]{3,2,1,0:T(8,128)S(1)} collective-permute-done((f32[16,1,32,128]{3,2,1,0:T(8,128)S(1)}, f32[16,1,32,128]{3,2,1,0:T(8,128)S(1)}, u32[]{:S(2)}, u32[]{:S(2)}) %collective-permute-start.9) | collective-permute-done | bytes 262176 | tf_op jit(solution)/shard_map/ppermute | solution.py:23
  113.2 4.5 %collective-permute-start.10 = (f32[16,18,1,128]{3,2,1,0:T(1,128)S(1)}, f32[16,18,1,128]{3,2,1,0:T(1,128)S(1)}, u32[]{:S(2)}, u32[]{:S(2)}) collective-permute-start(f32[16,18,1,128]{3,2,1,0:T(1,128)S(1)} %get-tuple-element.14), channel_id=1, source_target_pairs={{0,1},{1,2},{2,3},{3,4},{4,5},{5,6},{6,7},{8,9},{9,10},{10,11},{11... | collective-permute-start | bytes 442376 | tf_op jit(solution)/shard_map/ppermute | solution.py:22
  119.8 4.5 %constant_dynamic-update-slice_fusion.2 = f32[80,65536]{1,0:T(8,128)} fusion(f32[80,65536]{1,0:T(8,128)} %get-tuple-element.29, f32[2,8,512,128]{3,2,1,0:T(8,128)S(1)} %bitcast.74), kind=kLoop, calls=%fused_computation.174 | loop fusion | bytes 8388608
  124.3 4.4 %copy.28 = f32[2,8,512,128]{3,1,2,0:T(8,128)} copy(f32[2,8,512,128]{3,2,1,0:T(8,128)S(1)} %bitcast.75) | data formatting | bytes 8388608
  130.0 8.9 %select_maximum_fusion.4 = f32[16,18,34,130]{3,2,1,0:T(8,128)} fusion(f32[16,18,1,128]{3,2,1,0:T(1,128)S(1)} %collective-permute-done.11, f32[16,18,1,128]{3,2,1,0:T(1,128)S(1)} %collective-permute-done.10, f32[16,1,32,128]{3,2,1,0:T(8,128)S(1)} %collective-permute-done.9, f32[16,16,32,128]{3,2,1,0:T(8,128)S(1)} %fusion.34, ...), kind=kLoop, calls=%fused_computation.17 | loop fusion | flops 15275520 | bytes 10105344 | tf_op jit(solution)/shard_map/concatenate | solution.py:24
  138.8 8.1 %fusion.23 = f32[16,16,32,128]{3,2,1,0:T(8,128)S(1)} fusion(f32[16,18,34,130]{3,2,1,0:T(8,128)} %select_maximum_fusion.4, f32[16,18,1,128]{3,2,1,0:T(1,128)} %copy-done.16, f32[16,1,32,128]{3,2,1,0:T(8,128)} %copy-done.11, f32[16,16,32,128]{3,2,1,0:T(8,128)S(1)} %fusion.34, f32[16,1,32,128]{3,2,1,0:T(8,128)} %copy-done.10, f32[16,18,1,128]{3,2,1,0:T(1,128)} %copy-done.15, ...), kind=kLoop, calls=%fused_computation.60 | loop fusion | flops 22020096 | bytes 19496960 | tf_op jit(solution)/shard_map/jit(_where)/select_n | solution.py:46
  152.5 4.4 %constant_dynamic-update-slice_fusion.1 = f32[80,65536]{1,0:T(8,128)} fusion(f32[80,65536]{1,0:T(8,128)} %constant_dynamic-update-slice_fusion.2, f32[2,8,512,128]{3,2,1,0:T(8,128)S(1)} %bitcast.76), kind=kLoop, calls=%fused_computation.173 | loop fusion | bytes 8388608
  157.0 4.4 %copy.27 = f32[2,8,512,128]{3,1,2,0:T(8,128)} copy(f32[2,8,512,128]{3,2,1,0:T(8,128)S(1)} %bitcast.77) | data formatting | bytes 8388608
  167.4 4.4 %constant_dynamic-update-slice_fusion = f32[80,65536]{1,0:T(8,128)} fusion(f32[80,65536]{1,0:T(8,128)} %constant_dynamic-update-slice_fusion.1, f32[2,8,512,128]{3,2,1,0:T(8,128)S(1)} %bitcast.78), kind=kLoop, calls=%fused_computation.172 | loop fusion | bytes 8388608
  171.8 4.4 %copy.26 = f32[2,8,512,128]{3,1,2,0:T(8,128)} copy(f32[2,8,512,128]{3,2,1,0:T(8,128)S(1)} %bitcast.79) | data formatting | bytes 8388608
  176.2 9.0 %select_maximum_fusion = f32[16,18,34,130]{3,2,1,0:T(8,128)} fusion(f32[16,18,1,128]{3,2,1,0:T(1,128)S(1)} %collective-permute-done.15, f32[16,18,1,128]{3,2,1,0:T(1,128)S(1)} %collective-permute-done.14, f32[16,1,32,128]{3,2,1,0:T(8,128)S(1)} %collective-permute-done.13, f32[16,16,32,128]{3,2,1,0:T(8,128)S(1)} %fusion.23, ...), kind=kLoop, calls=%fused_computation.13 | loop fusion | flops 15275520 | bytes 10105344 | tf_op jit(solution)/shard_map/concatenate | solution.py:24
  185.2 10.9 %fusion.12 = f32[16,16,32,128]{3,2,1,0:T(8,128)S(1)} fusion(f32[16,18,34,130]{3,2,1,0:T(8,128)} %select_maximum_fusion, f32[16,18,1,128]{3,2,1,0:T(1,128)S(1)} %collective-permute-done.15, f32[16,1,32,128]{3,2,1,0:T(8,128)S(1)} %collective-permute-done.13, f32[16,16,32,128]{3,2,1,0:T(8,128)S(1)} %fusion.23, ...), kind=kLoop, calls=%fused_computation.39 | loop fusion | flops 22020096 | bytes 19496960 | tf_op jit(solution)/shard_map/jit(_where)/select_n | solution.py:46
  196.1 4.4 %bitcast_dynamic-update-slice_fusion = f32[80,65536]{1,0:T(8,128)} fusion(f32[80,65536]{1,0:T(8,128)} %constant_dynamic-update-slice_fusion, f32[2,8,512,128]{3,2,1,0:T(8,128)S(1)} %bitcast.87), kind=kLoop, calls=%fused_computation.32 | loop fusion | bytes 8388608 | tf_op jit(solution)/shard_map/concatenate | solution.py:91
  200.5 23.0 %fusion.85 = f32[80,80]{1,0:T(8,128)S(1)} fusion(f32[80,65536]{1,0:T(8,128)} %bitcast_dynamic-update-slice_fusion), kind=kOutput, calls=%fused_computation.182 | convolution fusion | flops 5033164800 | bytes 20997120 | tf_op jit(solution)/shard_map/dot_general | solution.py:92
  223.5 85.6 %psum.7 = f32[80,80]{1,0:T(8,128)S(1)} all-reduce(f32[80,80]{1,0:T(8,128)S(1)} %fusion.85), channel_id=1, replica_groups=mesh['gx'=32,'gy'=8] {'gx','gy'}, use_global_device_ids=true, to_apply=%region_0.1 | all-reduce | flops 6400 | bytes 51200 | tf_op jit(solution)/shard_map/psum | solution.py:92
  309.9 5.8 %cholesky.16 = f32[64,64]{1,0:T(8,128)S(1)} custom-call(f32[64,64]{1,0:T(8,128)S(1)} %fusion.73), custom_call_target="Cholesky" | custom-call | tf_op jit(solution)/shard_map/jit(cholesky)/cholesky | solution.py:63
  317.1 4.9 %custom-call.10 = f32[1,64,64]{1,2,0:T(8,128)S(1)} custom-call(f32[1,64,64]{2,1,0:T(8,128)S(1)} %fusion.68), custom_call_target="InvertDiagBlocksLowerTriangular" | custom-call | tf_op jit(solution)/shard_map/jit(_cho_solve)/triangular_solve | solution.py:64
  322.6 13.5 %fusion.57 = f32[2,8,512,128]{3,1,2,0:T(8,128)S(1)} fusion(f32[16,80]{1,0:T(8,128)S(1)} %fusion.88, f32[80,65536]{1,0:T(8,128)} %bitcast_dynamic-update-slice_fusion, f32[65536,16]{0,1:T(8,128)} %copy-done.2), kind=kOutput, calls=%fused_computation.125 | convolution fusion | flops 1007681536 | bytes 29365248 | tf_op jit(solution)/shard_map/dot_general | solution.py:96
  338.9 12.9 %fusion.54 = f32[2,8,512,128]{3,1,2,0:T(8,128)} fusion(f32[64,16]{0,1:T(8,128)S(1)} %fusion.69, f32[16,65536]{1,0:T(8,128)} %bitcast.90, f32[16,65536]{1,0:T(8,128)} %bitcast.89, f32[16,65536]{1,0:T(8,128)} %bitcast.88, f32[16,65536]{1,0:T(8,128)} %bitcast.86), kind=kOutput, calls=%fused_computation.124 | convolution fusion | flops 817889280 | bytes 20975616 | tf_op jit(solution)/shard_map/dot_general | solution.py:94
  351.8 5.0 %copy.14 = f32[2,8,512,128]{3,2,1,0:T(8,128)} copy(f32[2,8,512,128]{3,1,2,0:T(8,128)} %fusion.54) | data formatting | bytes 8388608
  (84 shorter events, 51.1 us)
Async XLA Ops:
  0.6 1.4 copy-start
  9.6 2.0 copy-start.2
  9.6 2.0 copy-start.17
  13.6 9.3 %collective-permute-start = (f32[17,1,32,128]{3,2,1,0:T(8,128)S(1)}, f32[17,1,32,128]{3,2,1,0:T(8,128)S(1)}, u32[]{:S(2)}, u32[]{:S(2)}) collective-permute-start(f32[17,1,32,128]{3,2,1,0:T(8,128)S(1)} %get-tuple-element.18), channel_id=1, source_target_pairs={{0,8},{8,16},{16,24},{24,32},{32,40},{40,48},{48,56},{56,64},{64,7... | collective-permute-start | bytes 835592 | tf_op jit(solution)/shard_map/ppermute | solution.py:22
  17.6 9.1 %collective-permute-start.1 = (f32[17,1,32,128]{3,2,1,0:T(8,128)S(1)}, f32[17,1,32,128]{3,2,1,0:T(8,128)S(1)}, u32[]{:S(2)}, u32[]{:S(2)}) collective-permute-start(f32[17,1,32,128]{3,2,1,0:T(8,128)S(1)} %get-tuple-element.19), channel_id=1, source_target_pairs={{8,0},{16,8},{24,16},{32,24},{40,32},{48,40},{56,48},{64,56},{72,6... | collective-permute-start | bytes 835592 | tf_op jit(solution)/shard_map/ppermute | solution.py:23
  22.9 16.8 %copy-start.8 = (f32[17,1,32,128]{3,2,1,0:T(8,128)}, f32[17,1,32,128]{3,2,1,0:T(8,128)S(1)}, u32[]{:S(2)}) copy-start(f32[17,1,32,128]{3,2,1,0:T(8,128)S(1)} %collective-permute-done) | copy-start | bytes 835588
  26.7 13.0 %copy-start.9 = (f32[17,1,32,128]{3,2,1,0:T(8,128)}, f32[17,1,32,128]{3,2,1,0:T(8,128)S(1)}, u32[]{:S(2)}) copy-start(f32[17,1,32,128]{3,2,1,0:T(8,128)S(1)} %collective-permute-done.1) | copy-start | bytes 835588
  26.9 7.1 %collective-permute-start.2 = (f32[17,18,1,128]{3,2,1,0:T(1,128)S(1)}, f32[17,18,1,128]{3,2,1,0:T(1,128)S(1)}, u32[]{:S(2)}, u32[]{:S(2)}) collective-permute-start(f32[17,18,1,128]{3,2,1,0:T(1,128)S(1)} %get-tuple-element.10), channel_id=1, source_target_pairs={{0,1},{1,2},{2,3},{3,4},{4,5},{5,6},{6,7},{8,9},{9,10},{10,11},{11... | collective-permute-start | bytes 470024 | tf_op jit(solution)/shard_map/ppermute | solution.py:22
  31.9 6.6 %collective-permute-start.3 = (f32[17,18,1,128]{3,2,1,0:T(1,128)S(1)}, f32[17,18,1,128]{3,2,1,0:T(1,128)S(1)}, u32[]{:S(2)}, u32[]{:S(2)}) collective-permute-start(f32[17,18,1,128]{3,2,1,0:T(1,128)S(1)} %get-tuple-element.11), channel_id=1, source_target_pairs={{1,0},{2,1},{3,2},{4,3},{5,4},{6,5},{7,6},{9,8},{10,9},{11,10},{12... | collective-permute-start | bytes 470024 | tf_op jit(solution)/shard_map/ppermute | solution.py:23
  34.1 5.6 %copy-start.12 = (f32[17,18,1,128]{3,2,1,0:T(1,128)}, f32[17,18,1,128]{3,2,1,0:T(1,128)S(1)}, u32[]{:S(2)}) copy-start(f32[17,18,1,128]{3,2,1,0:T(1,128)S(1)} %collective-permute-done.2) | copy-start | bytes 470020
  38.4 1.2 copy-start.13
  58.4 6.4 %collective-permute-start.4 = (f32[16,1,32,128]{3,2,1,0:T(8,128)S(1)}, f32[16,1,32,128]{3,2,1,0:T(8,128)S(1)}, u32[]{:S(2)}, u32[]{:S(2)}) collective-permute-start(f32[16,1,32,128]{3,2,1,0:T(8,128)S(1)} %get-tuple-element.24), channel_id=1, source_target_pairs={{0,8},{8,16},{16,24},{24,32},{32,40},{40,48},{48,56},{56,64},{64,7... | collective-permute-start | bytes 786440 | tf_op jit(solution)/shard_map/ppermute | solution.py:22
  61.5 7.4 %collective-permute-start.5 = (f32[16,1,32,128]{3,2,1,0:T(8,128)S(1)}, f32[16,1,32,128]{3,2,1,0:T(8,128)S(1)}, u32[]{:S(2)}, u32[]{:S(2)}) collective-permute-start(f32[16,1,32,128]{3,2,1,0:T(8,128)S(1)} %get-tuple-element.25), channel_id=1, source_target_pairs={{8,0},{16,8},{24,16},{32,24},{40,32},{48,40},{56,48},{64,56},{72,6... | collective-permute-start | bytes 786440 | tf_op jit(solution)/shard_map/ppermute | solution.py:23
  69.1 7.4 %collective-permute-start.6 = (f32[16,18,1,128]{3,2,1,0:T(1,128)S(1)}, f32[16,18,1,128]{3,2,1,0:T(1,128)S(1)}, u32[]{:S(2)}, u32[]{:S(2)}) collective-permute-start(f32[16,18,1,128]{3,2,1,0:T(1,128)S(1)} %get-tuple-element.16), channel_id=1, source_target_pairs={{0,1},{1,2},{2,3},{3,4},{4,5},{5,6},{6,7},{8,9},{9,10},{10,11},{11... | collective-permute-start | bytes 442376 | tf_op jit(solution)/shard_map/ppermute | solution.py:22
  74.3 15.5 %copy-start.3 = (f32[16,32,128]{2,1,0:T(8,128)S(1)}, f32[16,32,128]{2,1,0:T(8,128)}, u32[]{:S(2)}) copy-start(f32[16,32,128]{2,1,0:T(8,128)} %get-tuple-element.6) | copy-start | bytes 786436
  74.3 15.5 %copy-start.4 = (f32[16,32,128]{2,1,0:T(8,128)S(1)}, f32[16,32,128]{2,1,0:T(8,128)}, u32[]{:S(2)}) copy-start(f32[16,32,128]{2,1,0:T(8,128)} %get-tuple-element.7) | copy-start | bytes 786436
  74.3 15.5 %copy-start.6 = (f32[16,32,128]{2,1,0:T(8,128)S(1)}, f32[16,32,128]{2,1,0:T(8,128)}, u32[]{:S(2)}) copy-start(f32[16,32,128]{2,1,0:T(8,128)} %get-tuple-element.8) | copy-start | bytes 786436
  74.3 6.6 %collective-permute-start.7 = (f32[16,18,1,128]{3,2,1,0:T(1,128)S(1)}, f32[16,18,1,128]{3,2,1,0:T(1,128)S(1)}, u32[]{:S(2)}, u32[]{:S(2)}) collective-permute-start(f32[16,18,1,128]{3,2,1,0:T(1,128)S(1)} %get-tuple-element.17), channel_id=1, source_target_pairs={{1,0},{2,1},{3,2},{4,3},{5,4},{6,5},{7,6},{9,8},{10,9},{11,10},{12... | collective-permute-start | bytes 442376 | tf_op jit(solution)/shard_map/ppermute | solution.py:23
  100.7 7.8 %collective-permute-start.8 = (f32[16,1,32,128]{3,2,1,0:T(8,128)S(1)}, f32[16,1,32,128]{3,2,1,0:T(8,128)S(1)}, u32[]{:S(2)}, u32[]{:S(2)}) collective-permute-start(f32[16,1,32,128]{3,2,1,0:T(8,128)S(1)} %get-tuple-element.22), channel_id=1, source_target_pairs={{0,8},{8,16},{16,24},{24,32},{32,40},{40,48},{48,56},{56,64},{64,7... | collective-permute-start | bytes 786440 | tf_op jit(solution)/shard_map/ppermute | solution.py:22
  105.2 7.8 %collective-permute-start.9 = (f32[16,1,32,128]{3,2,1,0:T(8,128)S(1)}, f32[16,1,32,128]{3,2,1,0:T(8,128)S(1)}, u32[]{:S(2)}, u32[]{:S(2)}) collective-permute-start(f32[16,1,32,128]{3,2,1,0:T(8,128)S(1)} %get-tuple-element.23), channel_id=1, source_target_pairs={{8,0},{16,8},{24,16},{32,24},{40,32},{48,40},{56,48},{64,56},{72,6... | collective-permute-start | bytes 786440 | tf_op jit(solution)/shard_map/ppermute | solution.py:23
  108.5 20.2 %copy-start.10 = (f32[16,1,32,128]{3,2,1,0:T(8,128)}, f32[16,1,32,128]{3,2,1,0:T(8,128)S(1)}, u32[]{:S(2)}) copy-start(f32[16,1,32,128]{3,2,1,0:T(8,128)S(1)} %collective-permute-done.8) | copy-start | bytes 786436
  113.0 15.7 %copy-start.11 = (f32[16,1,32,128]{3,2,1,0:T(8,128)}, f32[16,1,32,128]{3,2,1,0:T(8,128)S(1)}, u32[]{:S(2)}) copy-start(f32[16,1,32,128]{3,2,1,0:T(8,128)S(1)} %collective-permute-done.9) | copy-start | bytes 786436
  113.2 15.5 %collective-permute-start.10 = (f32[16,18,1,128]{3,2,1,0:T(1,128)S(1)}, f32[16,18,1,128]{3,2,1,0:T(1,128)S(1)}, u32[]{:S(2)}, u32[]{:S(2)}) collective-permute-start(f32[16,18,1,128]{3,2,1,0:T(1,128)S(1)} %get-tuple-element.14), channel_id=1, source_target_pairs={{0,1},{1,2},{2,3},{3,4},{4,5},{5,6},{6,7},{8,9},{9,10},{10,11},{11... | collective-permute-start | bytes 442376 | tf_op jit(solution)/shard_map/ppermute | solution.py:22
  117.7 11.0 %collective-permute-start.11 = (f32[16,18,1,128]{3,2,1,0:T(1,128)S(1)}, f32[16,18,1,128]{3,2,1,0:T(1,128)S(1)}, u32[]{:S(2)}, u32[]{:S(2)}) collective-permute-start(f32[16,18,1,128]{3,2,1,0:T(1,128)S(1)} %get-tuple-element.15), channel_id=1, source_target_pairs={{1,0},{2,1},{3,2},{4,3},{5,4},{6,5},{7,6},{9,8},{10,9},{11,10},{12... | collective-permute-start | bytes 442376 | tf_op jit(solution)/shard_map/ppermute | solution.py:23
  128.7 10.2 %copy-start.5 = (f32[16,32,128]{2,1,0:T(8,128)S(1)}, f32[16,32,128]{2,1,0:T(8,128)}, u32[]{:S(2)}) copy-start(f32[16,32,128]{2,1,0:T(8,128)} %get-tuple-element.7) | copy-start | bytes 786436
  128.7 10.2 %copy-start.7 = (f32[16,32,128]{2,1,0:T(8,128)S(1)}, f32[16,32,128]{2,1,0:T(8,128)}, u32[]{:S(2)}) copy-start(f32[16,32,128]{2,1,0:T(8,128)} %get-tuple-element.8) | copy-start | bytes 786436
  147.0 14.3 %collective-permute-start.12 = (f32[16,1,32,128]{3,2,1,0:T(8,128)S(1)}, f32[16,1,32,128]{3,2,1,0:T(8,128)S(1)}, u32[]{:S(2)}, u32[]{:S(2)}) collective-permute-start(f32[16,1,32,128]{3,2,1,0:T(8,128)S(1)} %get-tuple-element.20), channel_id=1, source_target_pairs={{0,8},{8,16},{16,24},{24,32},{32,40},{40,48},{48,56},{56,64},{64,7... | collective-permute-start | bytes 786440 | tf_op jit(solution)/shard_map/ppermute | solution.py:22
  150.8 10.5 %collective-permute-start.13 = (f32[16,1,32,128]{3,2,1,0:T(8,128)S(1)}, f32[16,1,32,128]{3,2,1,0:T(8,128)S(1)}, u32[]{:S(2)}, u32[]{:S(2)}) collective-permute-start(f32[16,1,32,128]{3,2,1,0:T(8,128)S(1)} %get-tuple-element.21), channel_id=1, source_target_pairs={{8,0},{16,8},{24,16},{32,24},{40,32},{48,40},{56,48},{64,56},{72,6... | collective-permute-start | bytes 786440 | tf_op jit(solution)/shard_map/ppermute | solution.py:23
  161.5 14.7 %collective-permute-start.14 = (f32[16,18,1,128]{3,2,1,0:T(1,128)S(1)}, f32[16,18,1,128]{3,2,1,0:T(1,128)S(1)}, u32[]{:S(2)}, u32[]{:S(2)}) collective-permute-start(f32[16,18,1,128]{3,2,1,0:T(1,128)S(1)} %get-tuple-element.12), channel_id=1, source_target_pairs={{0,1},{1,2},{2,3},{3,4},{4,5},{5,6},{6,7},{8,9},{9,10},{10,11},{11... | collective-permute-start | bytes 442376 | tf_op jit(solution)/shard_map/ppermute | solution.py:22
  165.5 10.7 %collective-permute-start.15 = (f32[16,18,1,128]{3,2,1,0:T(1,128)S(1)}, f32[16,18,1,128]{3,2,1,0:T(1,128)S(1)}, u32[]{:S(2)}, u32[]{:S(2)}) collective-permute-start(f32[16,18,1,128]{3,2,1,0:T(1,128)S(1)} %get-tuple-element.13), channel_id=1, source_target_pairs={{1,0},{2,1},{3,2},{4,3},{5,4},{6,5},{7,6},{9,8},{10,9},{11,10},{12... | collective-permute-start | bytes 442376 | tf_op jit(solution)/shard_map/ppermute | solution.py:23
  200.5 108.7 %copy-start.14 = (f32[80,64]{1,0:T(8,128)S(1)}, f32[80,64]{1,0:T(8,128)}, u32[]{:S(2)}) copy-start(f32[80,64]{1,0:T(8,128)} %constant.62.clone) | copy-start | bytes 61444
  338.9 17.9 %copy-start.1 = (f32[16,64]{1,0:T(8,128)S(1)}, f32[16,64]{1,0:T(8,128)}, u32[]{:S(2)}) copy-start(f32[16,64]{1,0:T(8,128)} %param.10) | copy-start | bytes 12292
  (2 other events, 1.3 us)
where the time goes:
time: 364 us; the launch traced here: 357 us
  other arithmetic  91.4 us (25%)
  blocking collectives  85.6 us (24%)
  matrix products  58.2 us (16%)
  starting transfers between devices  47.6 us (13%)
  local copies, waits for them, and re-layouts  43.6 us (12%)
  waiting for transfers between devices  29.4 us (8%)
    psum x1, blocking collectives, shards(): gram = lax.psum(jnp.dot(flat, flat.T, precision=highest), ('gx', 'gy'))  85.6 us
    select_n x4, other arithmetic, neighbour_mean(): jnp.where(inside[None], summed / jnp.where(inside, weights, 1.0)[None], 0.0)  38.9 us
    unnamed x45, local copies, waits for them, and re-layouts  37.6 us
    concatenate x4, other arithmetic, with_halo(): value = jnp.concatenate([before, value, after], axis=dim)  36.4 us
    ppermute x8, starting transfers between devices, with_halo(): before = lax.ppermute(last, axis, up)  33.9 us
    dot_general x1, matrix products, shards(): gram = lax.psum(jnp.dot(flat, flat.T, precision=highest), ('gx', 'gy'))  23 us
    ppermute x8, waiting for transfers between devices, with_halo(): after = lax.ppermute(initial, axis, down)  21.1 us
    ppermute x8, starting transfers between devices, with_halo(): after = lax.ppermute(initial, axis, down)  13.8 us
  transfers between devices with their start and end apart: 16, of which 9 were waited for; matrix products, arithmetic and copies ran while one was open for 7% of the time, Pallas kernels for 0%

commit v1 on v0

v1 whole, which is shorter than its diff:
```python
import functools

import jax
import jax.numpy as jnp
from jax import lax
from jax.experimental import pallas as pl
from jax.experimental.pallas import tpu as pltpu
from jax.sharding import PartitionSpec as P

S = 4
NRHS = 16
LANES = 128
PAD = 8
CORES = 2
RING_X = 4
MESH = pl.DeviceIdType.MESH
F32 = jnp.float32
BF16 = jnp.bfloat16
ROWS = (S + 1) * NRHS
BASIS = S * NRHS


def split_hi_lo(value):
    high = value.astype(BF16)
    low = (value - high.astype(F32)).astype(BF16)
    return high, low


def krylov_kernel(nx, ny, phase_hbm, tab_hbm, source_hbm, sigma_ref, gain_ref, basis_hbm, total_ref,
                  phase_ext, tab_ext, source_ext, conduct, weight, f0, f1, f2, f3, basis, acc, packed,
                  part1, part2, part3, sum2, sum3,
                  own_sem, face_send, face_recv, basis_sem,
                  send1, recv1, send2, recv2, send3, recv3, send4, recv4):
    bx, by = phase_hbm.shape[0], phase_hbm.shape[1]
    ex = bx + 2 * S
    ey = by + 2 * S
    gx, gy = lax.axis_index("gx"), lax.axis_index("gy")
    xi, zi = lax.rem(gx, RING_X), lax.div(gx, RING_X)
    yi, ci = lax.div(gy, CORES), lax.rem(gy, CORES)
    ring_y = ny // CORES
    ring_z = nx // RING_X
    right, left = lax.rem(gx + 1, nx), lax.rem(gx + nx - 1, nx)
    up, down = lax.rem(gy + 1, ny), lax.rem(gy + ny - 1, ny)

    def at_y(o):
        return gx, lax.rem(gy + o, ny)

    def at_x(o):
        return zi * RING_X + lax.rem(xi + o, RING_X), gy

    def at_z(o):
        return lax.rem(zi + o, ring_z) * RING_X + xi, gy

    def at_row(o):
        return gx, lax.rem(yi + o, ring_y) * CORES + ci

    faces = ((right, gy), (left, gy), (right, up), (right, down), (left, up), (left, down))
    peers = faces + tuple(at_y(o) for o in range(1, ny)) + tuple(at_x(o) for o in range(1, RING_X)) + tuple(
        at_z(o) for o in range(1, ring_z))
    barrier = pltpu.get_barrier_semaphore()
    for peer in peers:
        pl.semaphore_signal(barrier, inc=1, device_id=peer, device_id_type=MESH)

    inputs = (phase_hbm, tab_hbm, source_hbm)
    wide = (phase_ext, tab_ext, source_ext)
    own_copies = []
    for a in range(3):
        copy = pltpu.make_async_copy(inputs[a], wide[a].at[pl.ds(S, bx), pl.ds(PAD, by)], own_sem.at[a])
        copy.start()
        own_copies.append(copy)
    for a in range(3):
        corner = jnp.zeros((PAD, LANES), wide[a].dtype)
        for x in (0, ex - 1):
            for y in (0, PAD + by):
                wide[a][x, y : y + PAD, :] = corner
    pl.semaphore_wait(barrier, len(peers))

    x_all, y_all = (0, bx), (0, by)
    x_top, x_low = (bx - S, S), (0, S)
    x_top3, x_low3 = (bx - S + 1, S - 1), (0, S - 1)
    y_top, y_low = (by - PAD, PAD), (0, PAD)
    routes = (
        ((gx, up), x_all, y_top, S, 0),
        ((gx, down), x_all, y_low, S, PAD + by),
        ((right, gy), x_top, y_all, 0, PAD),
        ((left, gy), x_low, y_all, S + bx, PAD),
        ((right, up), x_top3, y_top, 1, 0),
        ((right, down), x_top3, y_low, 1, PAD + by),
        ((left, up), x_low3, y_top, S + bx, 0),
        ((left, down), x_low3, y_low, S + bx, PAD + by),
    )
    face_copies = []
    for r, (peer, xs, ys, dx, dy) in enumerate(routes):
        for a in range(3):
            copy = pltpu.make_async_remote_copy(
                src_ref=inputs[a].at[pl.ds(*xs), pl.ds(*ys)],
                dst_ref=wide[a].at[pl.ds(dx, xs[1]), pl.ds(dy, ys[1])],
                send_sem=face_send.at[r, a],
                recv_sem=face_recv.at[r, a],
                device_id=peer,
                device_id_type=MESH,
            )
            copy.start()
            face_copies.append(copy)

    sigma0, sigma1, sigma2 = sigma_ref[0], sigma_ref[1], sigma_ref[2]
    gain = gain_ref[...]
    lane = lax.broadcasted_iota(jnp.int32, (PAD * 2 + by, LANES), 1)
    row_y = lax.broadcasted_iota(jnp.int32, (PAD * 2 + by, LANES), 0) + (gy * by - PAD)
    in_y = (row_y >= 0) & (row_y < ny * by)

    def start_columns(x, columns):
        for j in columns:
            tab = jnp.broadcast_to(tab_ext[x, pl.ds(j + PAD - S, 1), :], (NRHS, LANES))
            source = jnp.broadcast_to(source_ext[x, pl.ds(j + PAD - S, 1), :], (NRHS, LANES))
            picked = jnp.take_along_axis(gain, tab, axis=1, mode="promise_in_bounds")
            f0[x, j] = picked * source

    def mask_row(x):
        row_x = gx * bx + x - S
        inside = in_y & (row_x >= 0) & (row_x < nx * bx)
        phase = phase_ext[x]
        value = jnp.where(phase == 0, sigma0, jnp.where(phase == 1, sigma1, sigma2))
        conduct[x] = jnp.where(inside, value, 0.0)
        source_ext[x] = jnp.where(inside, source_ext[x], 0.0)

    def weight_row(x):
        c = conduct[x]
        zero = jnp.zeros_like(c)
        rows = by + 2 * PAD
        xm = c + conduct[x - 1]
        xp = c + conduct[x + 1]
        ym = c + pltpu.roll(c, 1, 0)
        yp = c + pltpu.roll(c, rows - 1, 0)
        low, top = lane > 0, lane < LANES - 1
        zm = c + jnp.where(low, pltpu.roll(c, 1, 1), zero)
        zp = c + jnp.where(top, pltpu.roll(c, LANES - 1, 1), zero)
        total = ((xm + xp) + (ym + yp)) + (zm + zp)
        inside = c > 0
        inverse = jnp.where(inside, 1.0 / jnp.where(inside, total, 1.0), 0.0)
        weight[0, x] = xm * inverse
        weight[1, x] = xp * inverse
        weight[2, x] = ym * inverse
        weight[3, x] = yp * inverse
        weight[4, x] = jnp.where(low, zm * inverse, zero)
        weight[5, x] = jnp.where(top, zp * inverse, zero)

    def mean_row(src, x, m, store):
        before, centre = src[x, m - 1], src[x, m]
        for j in range(m, ey - m):
            after = src[x, j + 1]
            w = [jnp.broadcast_to(weight[d, x, pl.ds(j + PAD - S, 1), :], (NRHS, LANES)) for d in range(6)]
            value = (w[0] * src[x - 1, j] + w[1] * src[x + 1, j]) + (w[2] * before + w[3] * after)
            value = value + (w[4] * pltpu.roll(centre, 1, 1) + w[5] * pltpu.roll(centre, LANES - 1, 1))
            store(j, value)
            before, centre = centre, after

    fields = (f0, f1, f2, f3)

    def inner_row(m):
        def body(x, carry):
            def store(j, value):
                fields[m][x, j] = value

            mean_row(fields[m - 1], x, m, store)
            return carry

        return body

    def last_row(x, carry):
        row = x - S

        def store(j, value):
            column = j - S
            values = [fields[m][x, j] for m in range(S)] + [value]
            for m in range(S + 1):
                high, low = split_hi_lo(values[m])
                basis[row, column, pl.ds(m * NRHS, NRHS), :] = high
                basis[row, column, pl.ds(ROWS + m * NRHS, NRHS), :] = low

        mean_row(fields[S - 1], x, S, store)
        pltpu.make_async_copy(basis.at[row], basis_hbm.at[row], basis_sem.at[row]).start()
        step = 8
        for first in range(0, by, step):
            block = jnp.concatenate([basis[row, first + k] for k in range(step)], axis=1)
            acc[...] += lax.dot_general(
                block[:ROWS], block, (((1,), (1,)), ((), ())), preferred_element_type=F32
            )
        return carry

    def rows_of(first, count, body):
        lax.fori_loop(first, first + count, body, 0)

    def two_sides(m, body):
        def both(r, carry):
            x = jnp.where(r < S, m + r, bx + S - m + r)
            return body(x, carry)

        return both

    for copy in own_copies:
        copy.wait()

    acc[...] = jnp.zeros_like(acc)

    def start_own(x, carry):
        start_columns(x, range(S, S + by))
        return carry

    rows_of(S, bx, start_own)
    for copy in face_copies[:6]:
        copy.wait_recv()

    def mask_own(x, carry):
        mask_row(x)
        start_columns(x, tuple(range(S)) + tuple(range(S + by, ey)))
        return carry

    def weight_own(x, carry):
        weight_row(x)
        return carry

    rows_of(S, bx, mask_own)
    rows_of(S + 1, bx - 2, weight_own)
    for m in range(1, S):
        rows_of(S + m, bx - 2 * m, inner_row(m))
    rows_of(2 * S, bx - 2 * S, last_row)

    for copy in face_copies[6:]:
        copy.wait_recv()

    def mask_far(x, carry):
        mask_row(x)
        start_columns(x, range(ey))
        return carry

    rows_of(0, S, mask_far)
    rows_of(S + bx, S, mask_far)
    rows_of(1, S, weight_own)
    rows_of(S + bx - 1, S, weight_own)
    for m in range(1, S):
        rows_of(m, S, inner_row(m))
        rows_of(S + bx - m, S, inner_row(m))
    rows_of(S, S, last_row)
    rows_of(bx, S, last_row)

    both = acc[...]
    lane_g = lax.broadcasted_iota(jnp.int32, (ROWS, LANES), 1)
    first = both[:, :LANES]
    second = jnp.concatenate([both[:, LANES:], jnp.zeros((ROWS, 2 * LANES - 2 * ROWS), F32)], axis=1)
    cross = pltpu.roll(jnp.where(lane_g >= ROWS, first, second), LANES - ROWS, 1)
    cross = jnp.where(lane_g < ROWS, cross, 0.0)
    square = jnp.concatenate([cross, jnp.zeros((LANES - ROWS, LANES), F32)], axis=0)
    gram = first + cross + square.T[:ROWS]
    lane_b = lane_g[:NRHS]
    blocks = [gram[m * NRHS : (m + 1) * NRHS] for m in range(S + 1)]
    top = jnp.where(lane_b < ROWS, blocks[0], pltpu.roll(blocks[2], 48, 1))
    low = jnp.where(
        lane_b < ROWS,
        blocks[1],
        jnp.where(lane_b < 112, pltpu.roll(blocks[3], 32, 1), pltpu.roll(blocks[4], 48, 1)),
    )
    packed[0] = top[:8]
    packed[1] = top[8:]
    packed[2] = low[:8]
    packed[3] = low[8:]

    def exchange(peers_of, source_of, slots, slot, send, recv):
        copies = []
        for k, peer in enumerate(peers_of):
            copy = pltpu.make_async_remote_copy(
                src_ref=source_of(peer),
                dst_ref=slots.at[slot],
                send_sem=send.at[k],
                recv_sem=recv.at[k],
                device_id=peer,
                device_id_type=MESH,
            )
            copy.start()
            copies.append(copy)
        for copy in copies:
            copy.wait()

    part1[gy] = packed[yi]
    exchange([at_y(o) for o in range(1, ny)], lambda peer: packed.at[lax.div(peer[1], CORES)], part1, gy, send1, recv1)
    sum2[...] = jnp.sum(part1[...], axis=0)
    part2[xi] = sum2[...]
    exchange([at_x(o) for o in range(1, RING_X)], lambda peer: sum2, part2, xi, send2, recv2)
    sum3[...] = jnp.sum(part2[...], axis=0)
    part3[zi] = sum3[...]
    exchange([at_z(o) for o in range(1, ring_z)], lambda peer: sum3, part3, zi, send3, recv3)
    total_ref[yi] = jnp.sum(part3[...], axis=0)
    exchange([at_row(o) for o in range(1, ring_y)], lambda peer: total_ref.at[yi], total_ref, yi, send4, recv4)

    for copy in face_copies:
        copy.wait_send()
    for row in range(bx):
        pltpu.make_async_copy(basis.at[row], basis_hbm.at[row], basis_sem.at[row]).wait()


def combine_kernel(basis_hbm, total_ref, sol_hbm, res_hbm, basis, sol, res, left_ref, basis_sem, sol_sem, res_sem):
    bx, by = basis_hbm.shape[0], basis_hbm.shape[1]

    def load(x):
        return pltpu.make_async_copy(basis_hbm.at[x], basis.at[x], basis_sem.at[x])

    for x in range(bx):
        load(x).start()

    top = jnp.concatenate([total_ref[0], total_ref[1]], axis=0)
    low = jnp.concatenate([total_ref[2], total_ref[3]], axis=0)
    blocks = [top, low, pltpu.roll(top, 80, 1), pltpu.roll(low, 96, 1), pltpu.roll(low, 80, 1)]
    upper = jnp.concatenate(blocks + [jnp.zeros((LANES - ROWS, LANES), F32)], axis=0)
    lane = lax.broadcasted_iota(jnp.int32, (LANES, LANES), 1)
    row = lax.broadcasted_iota(jnp.int32, (LANES, LANES), 0)
    keep = (lane // NRHS >= row // NRHS) & (lane < ROWS)
    upper = jnp.where(keep, upper, 0.0)
    gram = jnp.where(keep, upper, upper.T)
    down = gram[:BASIS] - gram[NRHS : BASIS + NRHS]
    lane64, row64 = lane[:BASIS], row[:BASIS]
    hess = down - pltpu.roll(down, LANES - NRHS, 1)
    work = jnp.where(lane64 < BASIS, hess, jnp.where(lane64 < ROWS, pltpu.roll(down, BASIS, 1), 0.0))
    for j in range(BASIS):
        pivot = work[j : j + 1, :]
        scaled = pivot / pivot[:, j : j + 1]
        column = work[:, j : j + 1]
        work = jnp.where(row64 == j, scaled, work - column * scaled)
    coeffs = jnp.where(lane64 < NRHS, pltpu.roll(work, LANES - BASIS, 1), 0.0)
    gap = jnp.zeros((NRHS, LANES), F32)
    full = jnp.concatenate([coeffs, gap], axis=0)
    moved = jnp.concatenate([gap, coeffs], axis=0)
    unit = jnp.where(lane[:ROWS] == row[:ROWS], 1.0, 0.0)
    unit = jnp.where(lane[:ROWS] < NRHS, unit, 0.0)
    other = unit - (full - moved)
    pair = full + pltpu.roll(other, NRHS, 1)
    tall = jnp.concatenate([pair, pair, jnp.zeros((2 * LANES - 2 * ROWS, LANES), F32)], axis=0)
    table = jnp.concatenate([tall[:LANES].T, tall[LANES:].T], axis=1)[: 2 * NRHS]
    high, low_part = split_hi_lo(table)
    left_ref[...] = jnp.concatenate([high, low_part], axis=0)
    left = left_ref[:, : 2 * ROWS]

    def body(x, carry):
        load(x).wait()
        for y in range(0, by, 2):
            right = jnp.concatenate([basis[x, y], basis[x, y + 1]], axis=1)
            both = jnp.dot(left, right, preferred_element_type=F32)
            both = both[: 2 * NRHS] + both[2 * NRHS :]
            for k in range(2):
                part = both[:, k * LANES : (k + 1) * LANES]
                sol[x, pl.ds(y + k, NRHS, stride=by), :] = part[:NRHS]
                res[x, pl.ds(y + k, NRHS, stride=by), :] = part[NRHS:]
        for p in range(NRHS):
            pltpu.make_async_copy(sol.at[x, pl.ds(p * by, by)], sol_hbm.at[p, x], sol_sem.at[x, p]).start()
            pltpu.make_async_copy(res.at[x, pl.ds(p * by, by)], res_hbm.at[p, x], res_sem.at[x, p]).start()
        return carry

    lax.fori_loop(0, bx, body, 0)

    def drain(x, carry):
        for p in range(NRHS):
            pltpu.make_async_copy(sol.at[x, pl.ds(p * by, by)], sol_hbm.at[p, x], sol_sem.at[x, p]).wait()
            pltpu.make_async_copy(res.at[x, pl.ds(p * by, by)], res_hbm.at[p, x], res_sem.at[x, p]).wait()
        return carry

    lax.fori_loop(0, bx, drain, 0)


def krylov_call(nx, ny, phase_label, tab_index, source_field, sigma_table, gain):
    bx, by = phase_label.shape[0], phase_label.shape[1]
    ex, ey = bx + 2 * S, by + 2 * S
    wide = (ex, by + 2 * PAD, LANES)
    ring_y, ring_z = ny // CORES, nx // RING_X
    hbm = pl.BlockSpec(memory_space=pl.ANY)
    vmem = pl.BlockSpec(memory_space=pltpu.VMEM)
    dma = pltpu.SemaphoreType.DMA
    tile = (8, LANES)
    return pl.pallas_call(
        functools.partial(krylov_kernel, nx, ny),
        out_shape=(
            jax.ShapeDtypeStruct((bx, by, 2 * ROWS, LANES), BF16),
            jax.ShapeDtypeStruct((ring_y,) + tile, F32),
        ),
        in_specs=[hbm, hbm, hbm, pl.BlockSpec(memory_space=pltpu.SMEM), vmem],
        out_specs=(hbm, vmem),
        scratch_shapes=[
            pltpu.VMEM(wide, jnp.int32),
            pltpu.VMEM(wide, jnp.int32),
            pltpu.VMEM(wide, F32),
            pltpu.VMEM(wide, F32),
            pltpu.VMEM((6,) + wide, F32),
        ]
        + [pltpu.VMEM((ex, ey, NRHS, LANES), F32)] * S
        + [
            pltpu.VMEM((bx, by, 2 * ROWS, LANES), BF16),
            pltpu.VMEM((ROWS, 2 * ROWS), F32),
            pltpu.VMEM((ring_y,) + tile, F32),
            pltpu.VMEM((ny,) + tile, F32),
            pltpu.VMEM((RING_X,) + tile, F32),
            pltpu.VMEM((ring_z,) + tile, F32),
            pltpu.VMEM(tile, F32),
            pltpu.VMEM(tile, F32),
            dma((3,)),
            dma((8, 3)),
            dma((8, 3)),
            dma((bx,)),
            dma((ny - 1,)),
            dma((ny - 1,)),
            dma((RING_X - 1,)),
            dma((RING_X - 1,)),
            dma((ring_z - 1,)),
            dma((ring_z - 1,)),
            dma((ring_y - 1,)),
            dma((ring_y - 1,)),
        ],
        compiler_params=pltpu.CompilerParams(
            collective_id=0, has_side_effects=True, vmem_limit_bytes=62 * 2**20
        ),
    )(phase_label, tab_index, source_field, sigma_table, gain)


def combine_call(basis, total):
    bx, by = basis.shape[0], basis.shape[1]
    hbm = pl.BlockSpec(memory_space=pl.ANY)
    vmem = pl.BlockSpec(memory_space=pltpu.VMEM)
    dma = pltpu.SemaphoreType.DMA
    out = jax.ShapeDtypeStruct((NRHS, bx, by, LANES), F32)
    return pl.pallas_call(
        combine_kernel,
        out_shape=(out, out),
        in_specs=[hbm, vmem],
        out_specs=(hbm, hbm),
        scratch_shapes=[
            pltpu.VMEM(basis.shape, BF16),
            pltpu.VMEM((bx, NRHS * by, LANES), F32),
            pltpu.VMEM((bx, NRHS * by, LANES), F32),
            pltpu.VMEM((4 * NRHS, 2 * LANES), BF16),
            dma((bx,)),
            dma((bx, NRHS)),
            dma((bx, NRHS)),
        ],
        compiler_params=pltpu.CompilerParams(vmem_limit_bytes=56 * 2**20),
    )(basis, total)


def solution(mesh):
    nx, ny = mesh.shape["gx"], mesh.shape["gy"]

    def shards(phase_label, tab_index, source_field, sigma_table, pattern_gain):
        gain = jnp.pad(pattern_gain, ((0, 0), (0, LANES - pattern_gain.shape[1])))
        basis, total = krylov_call(nx, ny, phase_label, tab_index, source_field, sigma_table, gain)
        return combine_call(basis, total)

    return jax.shard_map(
        shards,
        mesh=mesh,
        in_specs=(P("gx", "gy", None), P("gx", "gy", None), P("gx", "gy", None), P(), P()),
        out_specs=(P(None, "gx", "gy", None), P(None, "gx", "gy", None)),
        check_vma=False,
    )
```

time: 364 us -> 83.6 us (0.23); the launches traced: 357 us -> 82.7 us
  other arithmetic: 91.4 us -> 0 us
  blocking collectives: 85.6 us -> 0 us
  Pallas kernels: 0 us -> 80.8 us
  matrix products: 58.2 us -> 0 us
  starting transfers between devices: 47.6 us -> 0 us
  local copies, waits for them, and re-layouts: 43.6 us -> 1.3 us
  waiting for transfers between devices: 29.4 us -> 0 us
    psum x1 -> x0, blocking collectives: 85.6 us -> none  [shards(): gram = lax.psum(jnp.dot(flat, flat.T, precision=highest), ('gx', 'gy'))]
    pallas_call x0 -> x2, Pallas kernels: none -> 80.8 us  [the longest x1 59.9 us: krylov_call(): pl.pallas_call(functools.partial(krylov_kernel, nx, ny), out_shape=(jax.S...]
    dot_general x8 -> x0, matrix products: 57.8 us -> none  [the longest x1 23 us: shards(): gram = lax.psum(jnp.dot(flat, flat.T, precision=highest), ('gx', 'gy'))]
    ppermute x16 -> x0, starting transfers between devices: 47.6 us -> none  [the longest x8 33.9 us: with_halo(): before = lax.ppermute(last, axis, up)]
    select_n x5 -> x0, other arithmetic: 40.1 us -> none  [the longest x4 38.9 us: neighbour_mean(): jnp.where(inside[None], summed / jnp.where(inside, weights, 1.0)[None], 0.0)]
    unnamed x45 -> x0, local copies, waits for them, and re-layouts: 37.6 us -> none
    concatenate x4 -> x0, other arithmetic: 36.4 us -> none  [with_halo(): value = jnp.concatenate([before, value, after], axis=dim)]
    ppermute x16 -> x0, waiting for transfers between devices: 29.4 us -> none  [the longest x8 21.1 us: with_halo(): after = lax.ppermute(initial, axis, down)]
  transfers between devices with their start and end apart: 16 -> 0, of which waited for: 9 -> 0; matrix products, arithmetic and copies ran while one was open for 7% -> 0% of each run, Pallas kernels for 0% -> 0%
where the time goes in v1:
time: 83.6 us; the launch traced here: 82.7 us
  Pallas kernels  80.8 us (97%)
  local copies, waits for them, and re-layouts  1.3 us (2%)
    pallas_call x1, Pallas kernels, krylov_call(): pl.pallas_call(functools.partial(krylov_kernel, nx, ny), out_shape=(jax.S...  59.9 us
    pallas_call x1, Pallas kernels, combine_call(): pl.pallas_call(combine_kernel, out_shape=(out, out), in_specs=[hbm, vmem]...  20.9 us

profile of v1, /device:TPU:1, one launch (start us, length us, event | category | flops | bytes accessed | tf_op | source)
XLA Modules:
  0.0 82.7 jit_solution(12548502536187379087)
XLA Ops:
  0.6 1.3 %pad.4.gain_ref = f32[16,128]{1,0:T(8,128)} pad(f32[16,64]{1,0:T(8,128)} %param.9, f32[]{:T(128)} %constant.2.clone.1), padding=0_0x0_64 | pad | bytes 12292 | tf_op jit(solution)/shard_map/jit(_pad)/pad | solution.py:449
  1.9 59.9 %shard_map.68 = (bf16[16,32,160,128]{3,2,1,0:T(8,128)(2,1)}, f32[4,8,128]{2,1,0:T(8,128)}) custom-call(s32[16,32,128]{2,1,0:T(8,128)} %phase_hbm.1, s32[16,32,128]{2,1,0:T(8,128)} %tab_hbm.1, f32[16,32,128]{2,1,0:T(8,128)} %source_hbm.1, f32[3]{0:T(128)} %sigma_ref.1, f32[16,128]{1,0:T(8,128)} %pad.4.gain_ref), custom_call_target="tpu_custom_call" | custom-call | tf_op jit(solution)/shard_map/pallas_call | solution.py:377
  61.9 20.9 %shard_map.69 = (f32[16,16,32,128]{3,2,1,0:T(8,128)}, f32[16,16,32,128]{3,2,1,0:T(8,128)}) custom-call(bf16[16,32,160,128]{3,2,1,0:T(8,128)(2,1)} %get-tuple-element.4.basis_hbm, f32[4,8,128]{2,1,0:T(8,128)} %get-tuple-element.5.total_ref), custom_call_target="tpu_custom_call" | custom-call | tf_op jit(solution)/shard_map/pallas_call | solution.py:427

commit v2 on v1

v2 whole, which is shorter than its diff:
```python
import functools

import jax
import jax.numpy as jnp
from jax import lax
from jax.experimental import pallas as pl
from jax.experimental.pallas import tpu as pltpu
from jax.sharding import PartitionSpec as P

S = 4
NRHS = 16
LANES = 128
PAD = 8
RING_X = 4
MESH = pl.DeviceIdType.MESH
F32 = jnp.float32
BF16 = jnp.bfloat16
ROWS = (S + 1) * NRHS
BASIS = S * NRHS


def split_hi_lo(value):
    high = value.astype(BF16)
    low = (value - high.astype(F32)).astype(BF16)
    return high, low


def lane_pick(table, index):
    numbers = lax.GatherDimensionNumbers(
        offset_dims=(),
        collapsed_slice_dims=(1,),
        start_index_map=(1,),
        operand_batching_dims=(0,),
        start_indices_batching_dims=(0,),
    )
    return lax.gather(
        table, index[..., None], numbers, (1, 1), mode=lax.GatherScatterMode.PROMISE_IN_BOUNDS
    )


def krylov_kernel(nx, ny, phase_hbm, tab_hbm, source_hbm, sigma_ref, gain_ref, basis_hbm, total_ref,
                  phase_own, tab_ext, wide, conduct, charge, weight, f0, f1, f2, f3, f4, acc,
                  part1, part2, part3, own_sem, face_send, face_recv, basis_sem, ring_send, ring_recv):
    bx, by = phase_hbm.shape[0], phase_hbm.shape[1]
    ex = bx + 2 * S
    ey = by + 2 * S
    gx, gy = lax.axis_index("gx"), lax.axis_index("gy")
    xi, zi = lax.rem(gx, RING_X), lax.div(gx, RING_X)
    ring_z = nx // RING_X
    right, left = lax.rem(gx + 1, nx), lax.rem(gx + nx - 1, nx)
    up, down = lax.rem(gy + 1, ny), lax.rem(gy + ny - 1, ny)

    def at_y(o):
        return gx, lax.rem(gy + o, ny)

    def at_x(o):
        return zi * RING_X + lax.rem(xi + o, RING_X), gy

    def at_z(o):
        return lax.rem(zi + o, ring_z) * RING_X + xi, gy

    faces = ((right, gy), (left, gy), (right, up), (right, down), (left, up), (left, down))
    peers = faces + tuple(at_y(o) for o in range(1, ny)) + tuple(at_x(o) for o in range(1, RING_X)) + tuple(
        at_z(o) for o in range(1, ring_z))
    barrier = pltpu.get_barrier_semaphore()
    for peer in peers:
        pl.semaphore_signal(barrier, inc=1, device_id=peer, device_id_type=MESH)

    own = (pl.ds(S, bx), pl.ds(PAD, by))
    own_copies = [
        pltpu.make_async_copy(phase_hbm, phase_own, own_sem.at[0]),
        pltpu.make_async_copy(tab_hbm, tab_ext.at[own], own_sem.at[1]),
        pltpu.make_async_copy(source_hbm, wide.at[(2,) + own], own_sem.at[2]),
    ]
    for copy in own_copies:
        copy.start()
    corner = jnp.zeros((PAD, LANES), F32)
    for a in range(3):
        for x in (0, ex - 1):
            for y in (0, PAD + by):
                wide[a, x, y : y + PAD, :] = corner
    acc[...] = jnp.zeros_like(acc)
    sigma0, sigma1, sigma2 = sigma_ref[0], sigma_ref[1], sigma_ref[2]
    gain = jnp.concatenate([gain_ref[...], jnp.zeros((NRHS, LANES - gain_ref.shape[1]), F32)], axis=1)
    for copy in own_copies:
        copy.wait()

    def fill_row(r, carry):
        phase = phase_own[r]
        value = jnp.where(phase == 0, sigma0, jnp.where(phase == 1, sigma1, sigma2))
        wide[0, r + S, PAD : PAD + by, :] = value
        wide[1, r + S, PAD : PAD + by, :] = tab_ext[r + S, PAD : PAD + by, :].astype(F32)
        return carry

    lax.fori_loop(0, bx, fill_row, 0, unroll=4)
    pl.semaphore_wait(barrier, len(peers))

    x_all, y_all = (0, bx), (0, by)
    x_top, x_low = (bx - S, S), (0, S)
    x_top3, x_low3 = (bx - S + 1, S - 1), (0, S - 1)
    y_top, y_low = (by - PAD, PAD), (0, PAD)
    routes = (
        ((right, gy), x_top, y_all, 0, PAD),
        ((left, gy), x_low, y_all, S + bx, PAD),
        ((gx, up), x_all, y_top, S, 0),
        ((gx, down), x_all, y_low, S, PAD + by),
        ((right, up), x_top3, y_top, 1, 0),
        ((right, down), x_top3, y_low, 1, PAD + by),
        ((left, up), x_low3, y_top, S + bx, 0),
        ((left, down), x_low3, y_low, S + bx, PAD + by),
    )
    face_copies = []
    for r, (peer, xs, ys, dx, dy) in enumerate(routes):
        copy = pltpu.make_async_remote_copy(
            src_ref=wide.at[:, pl.ds(S + xs[0], xs[1]), pl.ds(PAD + ys[0], ys[1])],
            dst_ref=wide.at[:, pl.ds(dx, xs[1]), pl.ds(dy, ys[1])],
            send_sem=face_send.at[r],
            recv_sem=face_recv.at[r],
            device_id=peer,
            device_id_type=MESH,
        )
        copy.start()
        face_copies.append(copy)

    lane = lax.broadcasted_iota(jnp.int32, (PAD * 2 + by, LANES), 1)
    row_y = lax.broadcasted_iota(jnp.int32, (PAD * 2 + by, LANES), 0) + (gy * by - PAD)
    in_y = (row_y >= 0) & (row_y < ny * by)

    def start_columns(x, columns, strength):
        for j in columns:
            tab = jnp.broadcast_to(tab_ext[x, pl.ds(j + PAD - S, 1), :], (NRHS, LANES))
            f0[x, j] = lane_pick(gain, tab) * jnp.broadcast_to(strength(j + PAD - S), (NRHS, LANES))

    def start_own(x, carry):
        start_columns(x, range(S, S + by), lambda y: wide[2, x, pl.ds(y, 1), :])
        return carry

    def mask_row(x, sides):
        row_x = gx * bx + x - S
        inside = in_y & (row_x >= 0) & (row_x < nx * bx)
        conduct[x] = jnp.where(inside, wide[0, x], 0.0)
        charge[x] = jnp.where(inside, wide[2, x], 0.0)
        for first, count in sides:
            tab_ext[x, first : first + count, :] = wide[1, x, first : first + count, :].astype(jnp.int32)

    def mask_own(x, carry):
        mask_row(x, ((0, PAD), (PAD + by, PAD)))
        start_columns(x, tuple(range(S)) + tuple(range(S + by, ey)), lambda y: charge[x, pl.ds(y, 1), :])
        return carry

    def mask_far(x, carry):
        mask_row(x, ((0, 2 * PAD + by),))
        start_columns(x, range(ey), lambda y: charge[x, pl.ds(y, 1), :])
        return carry

    def weight_row(x, carry):
        c = conduct[x]
        zero = jnp.zeros_like(c)
        rows = by + 2 * PAD
        xm = c + conduct[x - 1]
        xp = c + conduct[x + 1]
        ym = c + pltpu.roll(c, 1, 0)
        yp = c + pltpu.roll(c, rows - 1, 0)
        low, top = lane > 0, lane < LANES - 1
        zm = c + jnp.where(low, pltpu.roll(c, 1, 1), zero)
        zp = c + jnp.where(top, pltpu.roll(c, LANES - 1, 1), zero)
        total = ((xm + xp) + (ym + yp)) + (zm + zp)
        inside = c > 0
        inverse = jnp.where(inside, 1.0 / jnp.where(inside, total, 1.0), 0.0)
        weight[0, x] = xm * inverse
        weight[1, x] = xp * inverse
        weight[2, x] = ym * inverse
        weight[3, x] = yp * inverse
        weight[4, x] = jnp.where(low, zm * inverse, zero)
        weight[5, x] = jnp.where(top, zp * inverse, zero)
        return carry

    def mean_rows(src, x, count, m, columns, before, centre, store):
        for j in columns:
            after = [src[x + r, j + 1] for r in range(count)]
            edge = [src[x - 1, j]] + centre + [src[x + count, j]]
            for r in range(count):
                w = [jnp.broadcast_to(weight[d, x + r, pl.ds(j + PAD - S, 1), :], (NRHS, LANES)) for d in range(6)]
                value = (w[0] * edge[r] + w[1] * edge[r + 2]) + (w[2] * before[r] + w[3] * after[r])
                value = value + (w[4] * pltpu.roll(centre[r], 1, 1) + w[5] * pltpu.roll(centre[r], LANES - 1, 1))
                store(r, j, value)
            before, centre = centre, after
        return before, centre

    fields = (f0, f1, f2, f3)

    def inner_rows(m, first):
        def body(i, carry):
            x = first + 2 * i

            def store(r, j, value):
                fields[m][x + r, j] = value

            src = fields[m - 1]
            before = [src[x + r, m - 1] for r in range(2)]
            centre = [src[x + r, m] for r in range(2)]
            mean_rows(src, x, 2, m, range(m, ey - m), before, centre, store)
            return carry

        return body

    def last_row(x, carry):
        row = x - S
        step = 8
        before, centre = [f3[x, S - 1]], [f3[x, S]]
        for first in range(S, S + by, step):
            newest = {}

            def store(r, j, value):
                newest[j] = value
                f4[row, j - S] = value

            before, centre = mean_rows(f3, x, 1, S, range(first, first + step), before, centre, store)
            columns = []
            for j in range(first, first + step):
                parts = [split_hi_lo(value) for value in [field[x, j] for field in fields] + [newest[j]]]
                columns.append(jnp.concatenate([p[0] for p in parts] + [p[1] for p in parts], axis=0))
            block = jnp.concatenate(columns, axis=1)
            acc[...] += lax.dot_general(
                block, block[:ROWS], (((1,), (1,)), ((), ())), preferred_element_type=F32
            )
        return carry

    def rows_of(first, count, body):
        lax.fori_loop(first, first + count, body, 0)

    def pairs_of(m, first, count):
        lax.fori_loop(0, count // 2, inner_rows(m, first), 0)

    def keep(m, first, count):
        src = f4.at[pl.ds(first, count)] if m == S else fields[m].at[pl.ds(S + first, count), pl.ds(S, by)]
        pltpu.make_async_copy(src, basis_hbm.at[m, pl.ds(first, count)], basis_sem).start()

    rows_of(S, bx, start_own)
    keep(0, 0, bx)
    for copy in face_copies[2:4]:
        copy.wait_recv()
    rows_of(S, bx, mask_own)
    rows_of(S + 1, bx - 2, weight_row)
    for m in range(1, S):
        pairs_of(m, S + m, bx - 2 * m)
        keep(m, m, bx - 2 * m)
    rows_of(2 * S, bx - 2 * S, last_row)
    keep(S, S, bx - 2 * S)

    for copy in face_copies[:2] + face_copies[4:]:
        copy.wait_recv()
    rows_of(0, S, mask_far)
    rows_of(S + bx, S, mask_far)
    rows_of(1, S, weight_row)
    rows_of(S + bx - 1, S, weight_row)
    for m in range(1, S):
        pairs_of(m, m, S)
        pairs_of(m, S + bx - m, S)
        keep(m, 0, m)
        keep(m, bx - m, m)
    rows_of(S, S, last_row)
    rows_of(bx, S, last_row)
    keep(S, 0, S)
    keep(S, bx - S, S)

    both = acc[...]
    both = both[:ROWS] + both[ROWS:]
    gram = jnp.concatenate([both, jnp.zeros((ROWS, LANES - ROWS), F32)], axis=1)
    lane_b = lax.broadcasted_iota(jnp.int32, (NRHS, LANES), 1)
    blocks = [gram[m * NRHS : (m + 1) * NRHS] for m in range(S + 1)]
    part1[gy, :NRHS] = blocks[0] + jnp.where(lane_b < ROWS, 0.0, pltpu.roll(blocks[2], 48, 1))
    part1[gy, NRHS:] = jnp.where(
        lane_b < ROWS,
        blocks[1],
        jnp.where(lane_b < 112, pltpu.roll(blocks[3], 32, 1), pltpu.roll(blocks[4], 48, 1)),
    )

    sends = []

    def spread(k, peers_of, slots, slot):
        copies = []
        for peer in peers_of:
            copy = pltpu.make_async_remote_copy(
                src_ref=slots.at[slot],
                dst_ref=slots.at[slot],
                send_sem=ring_send.at[k],
                recv_sem=ring_recv.at[k],
                device_id=peer,
                device_id_type=MESH,
            )
            copy.start()
            copies.append(copy)
        others = slots.at[pl.ds(0, len(copies))]
        whole = pltpu.make_async_copy(others, others, ring_recv.at[k])
        whole.wait()
        sends.append(pltpu.make_async_copy(others, others, ring_send.at[k]))
        return jnp.sum(slots[...], axis=0)

    part2[xi] = spread(0, [at_y(o) for o in range(1, ny)], part1, gy)
    part3[zi] = spread(1, [at_x(o) for o in range(1, RING_X)], part2, xi)
    total_ref[...] = spread(2, [at_z(o) for o in range(1, ring_z)], part3, zi)

    for send in sends:
        send.wait()
    for copy in face_copies:
        copy.wait_send()
    pltpu.make_async_copy(basis_hbm, basis_hbm, basis_sem).wait()


def solve_table(total):
    top, low = total[:NRHS], total[NRHS:]
    blocks = [top, low, pltpu.roll(top, 80, 1), pltpu.roll(low, 96, 1), pltpu.roll(low, 80, 1)]
    upper = jnp.concatenate(blocks + [jnp.zeros((LANES - ROWS, LANES), F32)], axis=0)
    lane = lax.broadcasted_iota(jnp.int32, (LANES, LANES), 1)
    row = lax.broadcasted_iota(jnp.int32, (LANES, LANES), 0)
    keep = (lane // NRHS >= row // NRHS) & (lane < ROWS)
    upper = jnp.where(keep, upper, 0.0)
    gram = jnp.where(keep, upper, upper.T)
    down = gram[:BASIS] - gram[NRHS : BASIS + NRHS]
    lane64, row64 = lane[:BASIS], row[:BASIS]
    hess = down - pltpu.roll(down, LANES - NRHS, 1)
    work = jnp.where(lane64 < BASIS, hess, jnp.where(lane64 < ROWS, pltpu.roll(down, BASIS, 1), 0.0))
    for j in range(BASIS):
        pivot = work[j : j + 1, :]
        scaled = pivot / pivot[:, j : j + 1]
        column = work[:, j : j + 1]
        work = jnp.where(row64 == j, scaled, work - column * scaled)
    coeffs = jnp.where(lane64 < NRHS, pltpu.roll(work, LANES - BASIS, 1), 0.0)
    gap = jnp.zeros((NRHS, LANES), F32)
    full = jnp.concatenate([coeffs, gap], axis=0)
    moved = jnp.concatenate([gap, coeffs], axis=0)
    unit = jnp.where((lane[:ROWS] == row[:ROWS]) & (lane[:ROWS] < NRHS), 1.0, 0.0)
    pair = full + pltpu.roll(unit - (full - moved), NRHS, 1)
    tall = jnp.concatenate([pair, pair, jnp.zeros((2 * LANES - 2 * ROWS, LANES), F32)], axis=0)
    return jnp.concatenate([tall[:LANES].T, tall[LANES:].T], axis=1)[: 2 * NRHS]


def combine_kernel(basis_hbm, total_ref, sol_hbm, res_hbm, basis, sol, res, left_ref, basis_sem, sol_sem, res_sem):
    bx, by = basis_hbm.shape[1], basis_hbm.shape[2]
    group = bx // basis_sem.shape[0]

    def load(g):
        rows = pl.ds(g * group, group)
        return pltpu.make_async_copy(basis_hbm.at[:, rows], basis.at[:, rows], basis_sem.at[g])

    for g in range(bx // group):
        load(g).start()

    high, low = split_hi_lo(solve_table(total_ref[...]))
    left_ref[...] = jnp.concatenate([high, low], axis=0)
    left = left_ref[:, : 2 * ROWS]

    def combine_row(x):
        for y in range(0, by, 2):
            columns = []
            for k in range(2):
                parts = [split_hi_lo(basis[m, x, y + k]) for m in range(S + 1)]
                columns.append(jnp.concatenate([p[0] for p in parts] + [p[1] for p in parts], axis=0))
            both = jnp.dot(left, jnp.concatenate(columns, axis=1), preferred_element_type=F32)
            both = both[: 2 * NRHS] + both[2 * NRHS :]
            for k in range(2):
                part = both[:, k * LANES : (k + 1) * LANES]
                sol.at[x].reshape(NRHS * by, LANES)[pl.ds(y + k, NRHS, stride=by), :] = part[:NRHS]
                res.at[x].reshape(NRHS * by, LANES)[pl.ds(y + k, NRHS, stride=by), :] = part[NRHS:]
        pltpu.make_async_copy(sol.at[x], sol_hbm.at[:, x], sol_sem).start()
        pltpu.make_async_copy(res.at[x], res_hbm.at[:, x], res_sem).start()

    def body(g, carry):
        load(g).wait()
        for r in range(group):
            combine_row(g * group + r)
        return carry

    lax.fori_loop(0, bx // group, body, 0)
    pltpu.make_async_copy(sol_hbm, sol_hbm, sol_sem).wait()
    pltpu.make_async_copy(res_hbm, res_hbm, res_sem).wait()


def krylov_call(nx, ny, phase_label, tab_index, source_field, sigma_table, gain):
    bx, by = phase_label.shape[0], phase_label.shape[1]
    ex, ey = bx + 2 * S, by + 2 * S
    wide = (ex, by + 2 * PAD, LANES)
    ring_z = nx // RING_X
    hbm = pl.BlockSpec(memory_space=pl.ANY)
    vmem = pl.BlockSpec(memory_space=pltpu.VMEM)
    dma = pltpu.SemaphoreType.DMA
    packed = (2 * NRHS, LANES)
    return pl.pallas_call(
        functools.partial(krylov_kernel, nx, ny),
        out_shape=(
            jax.ShapeDtypeStruct((S + 1, bx, by, NRHS, LANES), F32),
            jax.ShapeDtypeStruct(packed, F32),
        ),
        in_specs=[hbm, hbm, hbm, pl.BlockSpec(memory_space=pltpu.SMEM), vmem],
        out_specs=(hbm, vmem),
        scratch_shapes=[
            pltpu.VMEM((bx, by, LANES), jnp.int32),
            pltpu.VMEM(wide, jnp.int32),
            pltpu.VMEM((3,) + wide, F32),
            pltpu.VMEM(wide, F32),
            pltpu.VMEM(wide, F32),
            pltpu.VMEM((6,) + wide, F32),
        ]
        + [pltpu.VMEM((ex, ey, NRHS, LANES), F32)] * S
        + [
            pltpu.VMEM((bx, by, NRHS, LANES), F32),
            pltpu.VMEM((2 * ROWS, ROWS), F32),
            pltpu.VMEM((ny,) + packed, F32),
            pltpu.VMEM((RING_X,) + packed, F32),
            pltpu.VMEM((ring_z,) + packed, F32),
            dma((3,)),
            dma((8,)),
            dma((8,)),
            dma(()),
            dma((3,)),
            dma((3,)),
        ],
        compiler_params=pltpu.CompilerParams(
            collective_id=0, has_side_effects=True, vmem_limit_bytes=56 * 2**20
        ),
    )(phase_label, tab_index, source_field, sigma_table, gain)


def combine_call(basis, total):
    bx, by = basis.shape[1], basis.shape[2]
    hbm = pl.BlockSpec(memory_space=pl.ANY)
    vmem = pl.BlockSpec(memory_space=pltpu.VMEM)
    dma = pltpu.SemaphoreType.DMA
    out = jax.ShapeDtypeStruct((NRHS, bx, by, LANES), F32)
    return pl.pallas_call(
        combine_kernel,
        out_shape=(out, out),
        in_specs=[hbm, vmem],
        out_specs=(hbm, hbm),
        scratch_shapes=[
            pltpu.VMEM(basis.shape, F32),
            pltpu.VMEM((bx, NRHS, by, LANES), F32),
            pltpu.VMEM((bx, NRHS, by, LANES), F32),
            pltpu.VMEM((4 * NRHS, 2 * LANES), BF16),
            dma((bx // 2,)),
            dma(()),
            dma(()),
        ],
        compiler_params=pltpu.CompilerParams(vmem_limit_bytes=56 * 2**20),
    )(basis, total)


def solution(mesh):
    nx, ny = mesh.shape["gx"], mesh.shape["gy"]

    def shards(phase_label, tab_index, source_field, sigma_table, pattern_gain):
        basis, total = krylov_call(nx, ny, phase_label, tab_index, source_field, sigma_table, pattern_gain)
        return combine_call(basis, total)

    return jax.shard_map(
        shards,
        mesh=mesh,
        in_specs=(P("gx", "gy", None), P("gx", "gy", None), P("gx", "gy", None), P(), P()),
        out_specs=(P(None, "gx", "gy", None), P(None, "gx", "gy", None)),
        check_vma=False,
    )
```

time: 83.6 us -> 71.2 us (0.85)
  Pallas kernels: 80.8 us -> 70.3 us
  local copies, waits for them, and re-layouts: 1.3 us -> 0 us
    pallas_call x1, Pallas kernels: 20.9 us -> 15.6 us  [combine_call(): pl.pallas_call(combine_kernel, out_shape=(out, out), in_specs=[hbm, vmem]...]
    pallas_call x1, Pallas kernels: 59.9 us -> 54.7 us  [krylov_call(): pl.pallas_call(functools.partial(krylov_kernel, nx, ny), out_shape=(jax.S...]
    pad x1 -> x0, local copies, waits for them, and re-layouts: 1.3 us -> none  [shards(): gain = jnp.pad(pattern_gain, ((0, 0), (0, LANES - pattern_gain.shape[1])))]
where the time goes in v2:
time: 71.2 us; the launch traced here: 70.9 us
  Pallas kernels  70.3 us (99%)
    pallas_call x1, Pallas kernels, krylov_call(): pl.pallas_call(functools.partial(krylov_kernel, nx, ny), out_shape=(jax.S...  54.7 us
    pallas_call x1, Pallas kernels, combine_call(): pl.pallas_call(combine_kernel, out_shape=(out, out), in_specs=[hbm, vmem]...  15.6 us

profile of v2, /device:TPU:1, one launch (start us, length us, event | category | flops | bytes accessed | tf_op | source)
XLA Modules:
  0.0 70.9 jit_solution(2404206996722525876)
XLA Ops:
  0.6 54.7 %shard_map.68 = (f32[5,16,32,16,128]{4,3,2,1,0:T(8,128)}, f32[32,128]{1,0:T(8,128)}) custom-call(s32[16,32,128]{2,1,0:T(8,128)} %phase_hbm.1, s32[16,32,128]{2,1,0:T(8,128)} %tab_hbm.1, f32[16,32,128]{2,1,0:T(8,128)} %source_hbm.1, f32[3]{0:T(128)} %sigma_ref.1, f32[16,64]{1,0:T(8,128)} %gain_ref.1), custom_call_target="tpu_custom_call" | custom-call | tf_op jit(solution)/shard_map/pallas_call | solution.py:389
  55.4 15.6 %shard_map.69 = (f32[16,16,32,128]{3,2,1,0:T(8,128)}, f32[16,16,32,128]{3,2,1,0:T(8,128)}) custom-call(f32[5,16,32,16,128]{4,3,2,1,0:T(8,128)} %get-tuple-element.4.basis_hbm, f32[32,128]{1,0:T(8,128)} %get-tuple-element.5.total_ref), custom_call_target="tpu_custom_call" | custom-call | tf_op jit(solution)/shard_map/pallas_call | solution.py:431

commit v3 on v2

--- a/solution.py
+++ b/solution.py
@@ -222,7 +222,7 @@
                 columns.append(jnp.concatenate([p[0] for p in parts] + [p[1] for p in parts], axis=0))
             block = jnp.concatenate(columns, axis=1)
             acc[...] += lax.dot_general(
-                block, block[:ROWS], (((1,), (1,)), ((), ())), preferred_element_type=F32
+                block[:ROWS], block, (((1,), (1,)), ((), ())), preferred_element_type=F32
             )
         return carry
 
@@ -265,9 +265,14 @@
     keep(S, bx - S, S)
 
     both = acc[...]
-    both = both[:ROWS] + both[ROWS:]
-    gram = jnp.concatenate([both, jnp.zeros((ROWS, LANES - ROWS), F32)], axis=1)
-    lane_b = lax.broadcasted_iota(jnp.int32, (NRHS, LANES), 1)
+    lane_g = lax.broadcasted_iota(jnp.int32, (ROWS, LANES), 1)
+    first = both[:, :LANES]
+    second = jnp.concatenate([both[:, LANES:], jnp.zeros((ROWS, 2 * LANES - 2 * ROWS), F32)], axis=1)
+    cross = pltpu.roll(jnp.where(lane_g >= ROWS, first, second), LANES - ROWS, 1)
+    cross = jnp.where(lane_g < ROWS, cross, 0.0)
+    square = jnp.concatenate([cross, jnp.zeros((LANES - ROWS, LANES), F32)], axis=0)
+    gram = jnp.where(lane_g < ROWS, first, 0.0) + cross + square.T[:ROWS]
+    lane_b = lane_g[:NRHS]
     blocks = [gram[m * NRHS : (m + 1) * NRHS] for m in range(S + 1)]
     part1[gy, :NRHS] = blocks[0] + jnp.where(lane_b < ROWS, 0.0, pltpu.roll(blocks[2], 48, 1))
     part1[gy, NRHS:] = jnp.where(
@@ -339,6 +344,7 @@
 def combine_kernel(basis_hbm, total_ref, sol_hbm, res_hbm, basis, sol, res, left_ref, basis_sem, sol_sem, res_sem):
     bx, by = basis_hbm.shape[1], basis_hbm.shape[2]
     group = bx // basis_sem.shape[0]
+    pitch = sol.shape[2]
 
     def load(g):
         rows = pl.ds(g * group, group)
@@ -361,10 +367,10 @@
             both = both[: 2 * NRHS] + both[2 * NRHS :]
             for k in range(2):
                 part = both[:, k * LANES : (k + 1) * LANES]
-                sol.at[x].reshape(NRHS * by, LANES)[pl.ds(y + k, NRHS, stride=by), :] = part[:NRHS]
-                res.at[x].reshape(NRHS * by, LANES)[pl.ds(y + k, NRHS, stride=by), :] = part[NRHS:]
-        pltpu.make_async_copy(sol.at[x], sol_hbm.at[:, x], sol_sem).start()
-        pltpu.make_async_copy(res.at[x], res_hbm.at[:, x], res_sem).start()
+                sol.at[x].reshape(NRHS * pitch, LANES)[pl.ds(y + k, NRHS, stride=pitch), :] = part[:NRHS]
+                res.at[x].reshape(NRHS * pitch, LANES)[pl.ds(y + k, NRHS, stride=pitch), :] = part[NRHS:]
+        pltpu.make_async_copy(sol.at[x, :, pl.ds(0, by)], sol_hbm.at[:, x], sol_sem).start()
+        pltpu.make_async_copy(res.at[x, :, pl.ds(0, by)], res_hbm.at[:, x], res_sem).start()
 
     def body(g, carry):
         load(g).wait()
@@ -405,7 +411,7 @@
         + [pltpu.VMEM((ex, ey, NRHS, LANES), F32)] * S
         + [
             pltpu.VMEM((bx, by, NRHS, LANES), F32),
-            pltpu.VMEM((2 * ROWS, ROWS), F32),
+            pltpu.VMEM((ROWS, 2 * ROWS), F32),
             pltpu.VMEM((ny,) + packed, F32),
             pltpu.VMEM((RING_X,) + packed, F32),
             pltpu.VMEM((ring_z,) + packed, F32),
@@ -435,8 +441,8 @@
         out_specs=(hbm, hbm),
         scratch_shapes=[
             pltpu.VMEM(basis.shape, F32),
-            pltpu.VMEM((bx, NRHS, by, LANES), F32),
-            pltpu.VMEM((bx, NRHS, by, LANES), F32),
+            pltpu.VMEM((bx, NRHS, by + PAD, LANES), F32),
+            pltpu.VMEM((bx, NRHS, by + PAD, LANES), F32),
             pltpu.VMEM((4 * NRHS, 2 * LANES), BF16),
             dma((bx // 2,)),
             dma(()),

time: 71.2 us -> 68.4 us (0.961)
  Pallas kernels: 70.3 us -> 67.5 us
    pallas_call x1, Pallas kernels: 15.6 us -> 11.7 us  [combine_call(): pl.pallas_call(combine_kernel, out_shape=(out, out), in_specs=[hbm, vmem]...]
    pallas_call x1, Pallas kernels: 54.7 us -> 55.8 us  [krylov_call(): pl.pallas_call(functools.partial(krylov_kernel, nx, ny), out_shape=(jax.S...]
where the time goes in v3:
time: 68.4 us; the launch traced here: 68.1 us
  Pallas kernels  67.5 us (99%)
    pallas_call x1, Pallas kernels, krylov_call(): pl.pallas_call(functools.partial(krylov_kernel, nx, ny), out_shape=(jax.S...  55.8 us
    pallas_call x1, Pallas kernels, combine_call(): pl.pallas_call(combine_kernel, out_shape=(out, out), in_specs=[hbm, vmem]...  11.7 us

profile of v3, /device:TPU:1, one launch (start us, length us, event | category | flops | bytes accessed | tf_op | source)
XLA Modules:
  0.0 68.1 jit_solution(13268982822954124941)
XLA Ops:
  0.6 55.8 %shard_map.68 = (f32[5,16,32,16,128]{4,3,2,1,0:T(8,128)}, f32[32,128]{1,0:T(8,128)}) custom-call(s32[16,32,128]{2,1,0:T(8,128)} %phase_hbm.1, s32[16,32,128]{2,1,0:T(8,128)} %tab_hbm.1, f32[16,32,128]{2,1,0:T(8,128)} %source_hbm.1, f32[3]{0:T(128)} %sigma_ref.1, f32[16,64]{1,0:T(8,128)} %gain_ref.1), custom_call_target="tpu_custom_call" | custom-call | tf_op jit(solution)/shard_map/pallas_call | solution.py:395
  56.5 11.7 %shard_map.69 = (f32[16,16,32,128]{3,2,1,0:T(8,128)}, f32[16,16,32,128]{3,2,1,0:T(8,128)}) custom-call(f32[5,16,32,16,128]{4,3,2,1,0:T(8,128)} %get-tuple-element.4.basis_hbm, f32[32,128]{1,0:T(8,128)} %get-tuple-element.5.total_ref), custom_call_target="tpu_custom_call" | custom-call | tf_op jit(solution)/shard_map/pallas_call | solution.py:437

commit v4 on v3

--- a/solution.py
+++ b/solution.py
@@ -39,7 +39,7 @@
 
 
 def krylov_kernel(nx, ny, phase_hbm, tab_hbm, source_hbm, sigma_ref, gain_ref, basis_hbm, total_ref,
-                  phase_own, tab_ext, wide, conduct, charge, weight, f0, f1, f2, f3, f4, acc,
+                  phase_own, tab_ext, wide, conduct, charge, weight, f0, f1, f2, f3, f4, p0, p1, p2, acc,
                   part1, part2, part3, own_sem, face_send, face_recv, basis_sem, ring_send, ring_recv):
     bx, by = phase_hbm.shape[0], phase_hbm.shape[1]
     ex = bx + 2 * S
@@ -126,13 +126,25 @@
     row_y = lax.broadcasted_iota(jnp.int32, (PAD * 2 + by, LANES), 0) + (gy * by - PAD)
     in_y = (row_y >= 0) & (row_y < ny * by)
 
-    def start_columns(x, columns, strength):
+    fields = (f0, f1, f2, f3)
+    pieces = (p0, p1, p2)
+
+    def keep_pieces(m, row, column, value):
+        high, low = split_hi_lo(value)
+        pieces[m][row, column, :NRHS, :] = high
+        pieces[m][row, column, NRHS:, :] = low
+
+    def start_columns(x, columns, strength, row=None):
         for j in columns:
             tab = jnp.broadcast_to(tab_ext[x, pl.ds(j + PAD - S, 1), :], (NRHS, LANES))
-            f0[x, j] = lane_pick(gain, tab) * jnp.broadcast_to(strength(j + PAD - S), (NRHS, LANES))
+            value = lane_pick(gain, tab) * jnp.broadcast_to(strength(j + PAD - S), (NRHS, LANES))
+            f0[x, j] = value
+            if row is not None:
+                keep_pieces(0, row, j - S, value)
+            yield
 
     def start_own(x, carry):
-        start_columns(x, range(S, S + by), lambda y: wide[2, x, pl.ds(y, 1), :])
+        run(start_columns(x, range(S, S + by), lambda y: wide[2, x, pl.ds(y, 1), :], x - S))
         return carry
 
     def mask_row(x, sides):
@@ -145,13 +157,15 @@
 
     def mask_own(x, carry):
         mask_row(x, ((0, PAD), (PAD + by, PAD)))
-        start_columns(x, tuple(range(S)) + tuple(range(S + by, ey)), lambda y: charge[x, pl.ds(y, 1), :])
+        sides = tuple(range(S)) + tuple(range(S + by, ey))
+        run(start_columns(x, sides, lambda y: charge[x, pl.ds(y, 1), :]))
         return carry
 
-    def mask_far(x, carry):
-        mask_row(x, ((0, 2 * PAD + by),))
-        start_columns(x, range(ey), lambda y: charge[x, pl.ds(y, 1), :])
-        return carry
+    def start_far(rows):
+        for x in rows:
+            mask_row(x, ((0, 2 * PAD + by),))
+        for x in rows:
+            yield from start_columns(x, range(ey), lambda y, x=x: charge[x, pl.ds(y, 1), :])
 
     def weight_row(x, carry):
         c = conduct[x]
@@ -175,7 +189,9 @@
         weight[5, x] = jnp.where(top, zp * inverse, zero)
         return carry
 
-    def mean_rows(src, x, count, m, columns, before, centre, store):
+    def mean_rows(src, x, count, columns, store):
+        before = [src[x + r, columns[0] - 1] for r in range(count)]
+        centre = [src[x + r, columns[0]] for r in range(count)]
         for j in columns:
             after = [src[x + r, j + 1] for r in range(count)]
             edge = [src[x - 1, j]] + centre + [src[x + count, j]]
@@ -183,54 +199,77 @@
                 w = [jnp.broadcast_to(weight[d, x + r, pl.ds(j + PAD - S, 1), :], (NRHS, LANES)) for d in range(6)]
                 value = (w[0] * edge[r] + w[1] * edge[r + 2]) + (w[2] * before[r] + w[3] * after[r])
                 value = value + (w[4] * pltpu.roll(centre[r], 1, 1) + w[5] * pltpu.roll(centre[r], LANES - 1, 1))
-                store(r, j, value)
+                store(r, j, value, centre[r])
             before, centre = centre, after
-        return before, centre
-
-    fields = (f0, f1, f2, f3)
-
-    def inner_rows(m, first):
-        def body(i, carry):
-            x = first + 2 * i
-
-            def store(r, j, value):
-                fields[m][x + r, j] = value
-
-            src = fields[m - 1]
-            before = [src[x + r, m - 1] for r in range(2)]
-            centre = [src[x + r, m] for r in range(2)]
-            mean_rows(src, x, 2, m, range(m, ey - m), before, centre, store)
-            return carry
-
-        return body
-
-    def last_row(x, carry):
+            yield
+
+    def inner_pair(m, x, rows):
+        def store(r, j, value, centre):
+            fields[m][x + r, j] = value
+            if m < S - 1 and rows[r] is not None and S <= j < S + by:
+                keep_pieces(m, rows[r], j - S, value)
+
+        return mean_rows(fields[m - 1], x, 2, range(m, ey - m), store)
+
+    def far_pair(m, first, i):
+        rows = []
+        for r in range(2):
+            spots = [first + 2 * k + r - S for k in range(2)]
+            inside = [0 <= spot < bx for spot in spots]
+            spots = [spot if ok else bx for spot, ok in zip(spots, inside)]
+            rows.append(spots[0] + (spots[1] - spots[0]) * i if any(inside) else None)
+        return inner_pair(m, first + 2 * i, rows)
+
+    def last_row(x):
         row = x - S
         step = 8
-        before, centre = [f3[x, S - 1]], [f3[x, S]]
-        for first in range(S, S + by, step):
-            newest = {}
-
-            def store(r, j, value):
-                newest[j] = value
-                f4[row, j - S] = value
-
-            before, centre = mean_rows(f3, x, 1, S, range(first, first + step), before, centre, store)
-            columns = []
-            for j in range(first, first + step):
-                parts = [split_hi_lo(value) for value in [field[x, j] for field in fields] + [newest[j]]]
-                columns.append(jnp.concatenate([p[0] for p in parts] + [p[1] for p in parts], axis=0))
-            block = jnp.concatenate(columns, axis=1)
-            acc[...] += lax.dot_general(
-                block[:ROWS], block, (((1,), (1,)), ((), ())), preferred_element_type=F32
-            )
-        return carry
+        columns = []
+
+        def store(r, j, value, centre):
+            f4[row, j - S] = value
+            parts = [split_hi_lo(centre), split_hi_lo(value)]
+            highs = [p[row, j - S, :NRHS, :] for p in pieces] + [p[0] for p in parts]
+            lows = [p[row, j - S, NRHS:, :] for p in pieces] + [p[1] for p in parts]
+            columns.append(jnp.concatenate(highs + lows, axis=0))
+
+        for _ in mean_rows(f3, x, 1, range(S, S + by), store):
+            if len(columns) == step:
+                block = jnp.concatenate(columns, axis=1)
+                acc[...] += lax.dot_general(
+                    block[:ROWS], block, (((1,), (1,)), ((), ())), preferred_element_type=F32
+                )
+                columns.clear()
+            yield
+
+    def run(work):
+        for _ in work:
+            pass
+
+    def weave(work, count, other, extra):
+        done = 0
+        for k, _ in enumerate(work):
+            while done * count < extra * (k + 1):
+                next(other, None)
+                done += 1
+        run(other)
 
     def rows_of(first, count, body):
         lax.fori_loop(first, first + count, body, 0)
 
-    def pairs_of(m, first, count):
-        lax.fori_loop(0, count // 2, inner_rows(m, first), 0)
+    def pairs_of(m):
+        def body(i, carry):
+            x = S + m + 2 * i
+            run(inner_pair(m, x, (x - S, x + 1 - S)))
+            return carry
+
+        lax.fori_loop(0, bx // 2 - m, body, 0)
+
+    def twice(work):
+        def body(i, carry):
+            work(i)
+            return carry
+
+        lax.fori_loop(0, 2, body, 0)
 
     def keep(m, first, count):
         src = f4.at[pl.ds(first, count)] if m == S else fields[m].at[pl.ds(S + first, count), pl.ds(S, by)]
@@ -243,25 +282,35 @@
     rows_of(S, bx, mask_own)
     rows_of(S + 1, bx - 2, weight_row)
     for m in range(1, S):
-        pairs_of(m, S + m, bx - 2 * m)
+        pairs_of(m)
         keep(m, m, bx - 2 * m)
-    rows_of(2 * S, bx - 2 * S, last_row)
-    keep(S, S, bx - 2 * S)
 
     for copy in face_copies[:2] + face_copies[4:]:
         copy.wait_recv()
-    rows_of(0, S, mask_far)
-    rows_of(S + bx, S, mask_far)
+    low, top, inner = S, bx, 2 * S
+    wide_pair = 2 * ey
+    twice(lambda i: weave(last_row(inner + i), by, start_far((2 * i, 2 * i + 1)), wide_pair))
     rows_of(1, S, weight_row)
-    rows_of(S + bx - 1, S, weight_row)
+    twice(lambda i: weave(last_row(inner + 2 + i), by, far_pair(1, 1, i), ey - 2))
+    twice(lambda i: weave(last_row(inner + 4 + i), by, far_pair(2, 2, i), ey - 4))
+    far = S + bx
+    twice(lambda i: weave(last_row(inner + 6 + i), by, start_far((far + 2 * i, far + 2 * i + 1)), wide_pair))
+    keep(S, S, bx - 2 * S)
+    rows_of(far - 1, S, weight_row)
+    twice(lambda i: run(far_pair(3, 3, i)))
+    twice(lambda i: weave(last_row(low + i), by, far_pair(1, far - 1, i), ey - 2))
+    twice(lambda i: weave(last_row(low + 2 + i), by, far_pair(2, far - 2, i), ey - 4))
+    keep(S, 0, S)
+    twice(lambda i: run(far_pair(3, far - 3, i)))
     for m in range(1, S):
-        pairs_of(m, m, S)
-        pairs_of(m, S + bx - m, S)
         keep(m, 0, m)
         keep(m, bx - m, m)
-    rows_of(S, S, last_row)
-    rows_of(bx, S, last_row)
-    keep(S, 0, S)
+
+    def last_top(x, carry):
+        run(last_row(x))
+        return carry
+
+    rows_of(top, S, last_top)
     keep(S, bx - S, S)
 
     both = acc[...]
@@ -411,6 +460,9 @@
         + [pltpu.VMEM((ex, ey, NRHS, LANES), F32)] * S
         + [
             pltpu.VMEM((bx, by, NRHS, LANES), F32),
+            pltpu.VMEM((bx + 1, by, 2 * NRHS, LANES), BF16),
+            pltpu.VMEM((bx + 1, by, 2 * NRHS, LANES), BF16),
+            pltpu.VMEM((bx + 1, by, 2 * NRHS, LANES), BF16),
             pltpu.VMEM((ROWS, 2 * ROWS), F32),
             pltpu.VMEM((ny,) + packed, F32),
             pltpu.VMEM((RING_X,) + packed, F32),
@@ -423,7 +475,7 @@
             dma((3,)),
         ],
         compiler_params=pltpu.CompilerParams(
-            collective_id=0, has_side_effects=True, vmem_limit_bytes=56 * 2**20
+            collective_id=0, has_side_effects=True, vmem_limit_bytes=60 * 2**20
         ),
     )(phase_label, tab_index, source_field, sigma_table, gain)
 

time: 68.4 us -> 64 us (0.936)
  Pallas kernels: 67.5 us -> 63.1 us
    pallas_call x1, Pallas kernels: 55.8 us -> 51.4 us  [krylov_call(): pl.pallas_call(functools.partial(krylov_kernel, nx, ny), out_shape=(jax.S...]
where the time goes in v4:
time: 64 us; the launch traced here: 63.7 us
  Pallas kernels  63.1 us (99%)
  between operations  0.64 us (1%)
    pallas_call x1, Pallas kernels, krylov_call(): pl.pallas_call(functools.partial(krylov_kernel, nx, ny), out_shape=(jax.S...  51.4 us
    pallas_call x1, Pallas kernels, combine_call(): pl.pallas_call(combine_kernel, out_shape=(out, out), in_specs=[hbm, vmem]...  11.7 us

profile of v4, /device:TPU:1, one launch (start us, length us, event | category | flops | bytes accessed | tf_op | source)
XLA Modules:
  0.0 63.7 jit_solution(14176281051274455515)
XLA Ops:
  0.6 51.4 %shard_map.68 = (f32[5,16,32,16,128]{4,3,2,1,0:T(8,128)}, f32[32,128]{1,0:T(8,128)}) custom-call(s32[16,32,128]{2,1,0:T(8,128)} %phase_hbm.1, s32[16,32,128]{2,1,0:T(8,128)} %tab_hbm.1, f32[16,32,128]{2,1,0:T(8,128)} %source_hbm.1, f32[3]{0:T(128)} %sigma_ref.1, f32[16,64]{1,0:T(8,128)} %gain_ref.1), custom_call_target="tpu_custom_call" | custom-call | tf_op jit(solution)/shard_map/pallas_call | solution.py:444
  52.0 11.7 %shard_map.69 = (f32[16,16,32,128]{3,2,1,0:T(8,128)}, f32[16,16,32,128]{3,2,1,0:T(8,128)}) custom-call(f32[5,16,32,16,128]{4,3,2,1,0:T(8,128)} %get-tuple-element.4.basis_hbm, f32[32,128]{1,0:T(8,128)} %get-tuple-element.5.total_ref), custom_call_target="tpu_custom_call" | custom-call | tf_op jit(solution)/shard_map/pallas_call | solution.py:489

commit v5 on v4

--- a/solution.py
+++ b/solution.py
@@ -59,13 +59,6 @@
     def at_z(o):
         return lax.rem(zi + o, ring_z) * RING_X + xi, gy
 
-    faces = ((right, gy), (left, gy), (right, up), (right, down), (left, up), (left, down))
-    peers = faces + tuple(at_y(o) for o in range(1, ny)) + tuple(at_x(o) for o in range(1, RING_X)) + tuple(
-        at_z(o) for o in range(1, ring_z))
-    barrier = pltpu.get_barrier_semaphore()
-    for peer in peers:
-        pl.semaphore_signal(barrier, inc=1, device_id=peer, device_id_type=MESH)
-
     own = (pl.ds(S, bx), pl.ds(PAD, by))
     own_copies = [
         pltpu.make_async_copy(phase_hbm, phase_own, own_sem.at[0]),
@@ -74,6 +67,12 @@
     ]
     for copy in own_copies:
         copy.start()
+    faces = ((right, gy), (left, gy), (right, up), (right, down), (left, up), (left, down))
+    peers = faces + tuple(at_y(o) for o in range(1, ny)) + tuple(at_x(o) for o in range(1, RING_X)) + tuple(
+        at_z(o) for o in range(1, ring_z))
+    barrier = pltpu.get_barrier_semaphore()
+    for peer in peers:
+        pl.semaphore_signal(barrier, inc=1, device_id=peer, device_id_type=MESH)
     corner = jnp.zeros((PAD, LANES), F32)
     for a in range(3):
         for x in (0, ex - 1):
@@ -89,10 +88,177 @@
         phase = phase_own[r]
         value = jnp.where(phase == 0, sigma0, jnp.where(phase == 1, sigma1, sigma2))
         wide[0, r + S, PAD : PAD + by, :] = value
+        conduct[r + S, PAD : PAD + by, :] = value
         wide[1, r + S, PAD : PAD + by, :] = tab_ext[r + S, PAD : PAD + by, :].astype(F32)
         return carry
 
     lax.fori_loop(0, bx, fill_row, 0, unroll=4)
+    lane = lax.broadcasted_iota(jnp.int32, (PAD * 2 + by, LANES), 1)
+    row_y = lax.broadcasted_iota(jnp.int32, (PAD * 2 + by, LANES), 0) + (gy * by - PAD)
+    in_y = (row_y >= 0) & (row_y < ny * by)
+
+    fields = (f0, f1, f2, f3)
+    pieces = (p0, p1, p2)
+
+    def keep_pieces(m, row, column, value):
+        high, low = split_hi_lo(value)
+        pieces[m][row, column, :NRHS, :] = high
+        pieces[m][row, column, NRHS:, :] = low
+
+    def start_columns(x, columns, strength, row=None):
+        for j in columns:
+            tab = jnp.broadcast_to(tab_ext[x, pl.ds(j + PAD - S, 1), :], (NRHS, LANES))
+            value = lane_pick(gain, tab) * jnp.broadcast_to(strength(j + PAD - S), (NRHS, LANES))
+            f0[x, j] = value
+            if row is not None:
+                keep_pieces(0, row, j - S, value)
+            yield
+
+    def start_own(x, carry):
+        run(start_columns(x, range(S, S + by), lambda y: wide[2, x, pl.ds(y, 1), :], x - S))
+        return carry
+
+    def mask_row(x, sides):
+        row_x = gx * bx + x - S
+        in_x = (row_x >= 0) & (row_x < nx * bx)
+        for first, count in sides:
+            at = slice(first, first + count)
+            inside = in_y[at] & in_x
+            conduct[x, at, :] = jnp.where(inside, wide[0, x, at, :], 0.0)
+            charge[x, at, :] = jnp.where(inside, wide[2, x, at, :], 0.0)
+            tab_ext[x, at, :] = wide[1, x, at, :].astype(jnp.int32)
+
+    def mask_own(x, carry):
+        mask_row(x, ((0, PAD), (PAD + by, PAD)))
+        sides = tuple(range(S)) + tuple(range(S + by, ey))
+        run(start_columns(x, sides, lambda y: charge[x, pl.ds(y, 1), :]))
+        return carry
+
+    def start_far(rows):
+        for x in rows:
+            mask_row(x, ((0, 2 * PAD + by),))
+        for x in rows:
+            yield from start_columns(x, range(ey), lambda y, x=x: charge[x, pl.ds(y, 1), :])
+
+    def weight_part(x, first, count, start, stop):
+        at = slice(first, first + count)
+        c = conduct[x, at, :]
+        zero = jnp.zeros_like(c)
+        xm = c + conduct[x - 1, at, :]
+        xp = c + conduct[x + 1, at, :]
+        ym = c + pltpu.roll(c, 1, 0)
+        yp = c + pltpu.roll(c, count - 1, 0)
+        low, top = lane[at] > 0, lane[at] < LANES - 1
+        zm = c + jnp.where(low, pltpu.roll(c, 1, 1), zero)
+        zp = c + jnp.where(top, pltpu.roll(c, LANES - 1, 1), zero)
+        total = ((xm + xp) + (ym + yp)) + (zm + zp)
+        inside = c > 0
+        inverse = jnp.where(inside, 1.0 / jnp.where(inside, total, 1.0), 0.0)
+        parts = (xm, xp, ym, yp, jnp.where(low, zm, zero), jnp.where(top, zp, zero))
+        for d, part in enumerate(parts):
+            weight[d, x, start:stop, :] = (part * inverse)[start - first : stop - first]
+
+    def weight_row(x, carry):
+        weight_part(x, 0, by + 2 * PAD, 0, by + 2 * PAD)
+        return carry
+
+    def weight_inner(x, carry):
+        weight_part(x, PAD, by, PAD, PAD + by)
+        return carry
+
+    def weight_sides(x, carry):
+        weight_part(x, 0, 2 * PAD, 0, PAD + 1)
+        weight_part(x, by, 2 * PAD, PAD + by - 1, by + 2 * PAD)
+        return carry
+
+    def mean_rows(src, x, count, columns, store):
+        before = [src[x + r, columns[0] - 1] for r in range(count)]
+        centre = [src[x + r, columns[0]] for r in range(count)]
+        for j in columns:
+            after = [src[x + r, j + 1] for r in range(count)]
+            edge = [src[x - 1, j]] + centre + [src[x + count, j]]
+            for r in range(count):
+                w = [jnp.broadcast_to(weight[d, x + r, pl.ds(j + PAD - S, 1), :], (NRHS, LANES)) for d in range(6)]
+                value = (w[0] * edge[r] + w[1] * edge[r + 2]) + (w[2] * before[r] + w[3] * after[r])
+                value = value + (w[4] * pltpu.roll(centre[r], 1, 1) + w[5] * pltpu.roll(centre[r], LANES - 1, 1))
+                store(r, j, value, centre[r])
+            before, centre = centre, after
+            yield
+
+    def inner_pair(m, x, rows, columns=None):
+        def store(r, j, value, centre):
+            fields[m][x + r, j] = value
+            if m < S - 1 and rows[r] is not None and S <= j < S + by:
+                keep_pieces(m, rows[r], j - S, value)
+
+        return mean_rows(fields[m - 1], x, 2, range(m, ey - m) if columns is None else columns, store)
+
+    def far_pair(m, first, i):
+        rows = []
+        for r in range(2):
+            spots = [first + 2 * k + r - S for k in range(2)]
+            inside = [0 <= spot < bx for spot in spots]
+            spots = [spot if ok else bx for spot, ok in zip(spots, inside)]
+            rows.append(spots[0] + (spots[1] - spots[0]) * i if any(inside) else None)
+        return inner_pair(m, first + 2 * i, rows)
+
+    def last_row(x):
+        row = x - S
+        step = 8
+        columns = []
+
+        def store(r, j, value, centre):
+            f4[row, j - S] = value
+            parts = [split_hi_lo(centre), split_hi_lo(value)]
+            highs = [p[row, j - S, :NRHS, :] for p in pieces] + [p[0] for p in parts]
+            lows = [p[row, j - S, NRHS:, :] for p in pieces] + [p[1] for p in parts]
+            columns.append(jnp.concatenate(highs + lows, axis=0))
+
+        for _ in mean_rows(f3, x, 1, range(S, S + by), store):
+            if len(columns) == step:
+                block = jnp.concatenate(columns, axis=1)
+                acc[...] += lax.dot_general(
+                    block[:ROWS], block, (((1,), (1,)), ((), ())), preferred_element_type=F32
+                )
+                columns.clear()
+            yield
+
+    def run(work):
+        for _ in work:
+            pass
+
+    def weave(work, count, other, extra):
+        done = 0
+        for k, _ in enumerate(work):
+            while done * count < extra * (k + 1):
+                next(other, None)
+                done += 1
+        run(other)
+
+    def rows_of(first, count, body):
+        lax.fori_loop(first, first + count, body, 0, unroll=2)
+
+    def pairs_of(m, *parts):
+        def body(i, carry):
+            x = S + m + 2 * i
+            for columns in parts:
+                run(inner_pair(m, x, (x - S, x + 1 - S), columns))
+            return carry
+
+        lax.fori_loop(0, bx // 2 - m, body, 0)
+
+    def twice(work):
+        def body(i, carry):
+            work(i)
+            return carry
+
+        lax.fori_loop(0, 2, body, 0)
+
+    def keep(m, first, count):
+        src = f4.at[pl.ds(first, count)] if m == S else fields[m].at[pl.ds(S + first, count), pl.ds(S, by)]
+        pltpu.make_async_copy(src, basis_hbm.at[m, pl.ds(first, count)], basis_sem).start()
+
+    rows_of(S, bx, start_own)
     pl.semaphore_wait(barrier, len(peers))
 
     x_all, y_all = (0, bx), (0, by)
@@ -121,168 +287,17 @@
         )
         copy.start()
         face_copies.append(copy)
-
-    lane = lax.broadcasted_iota(jnp.int32, (PAD * 2 + by, LANES), 1)
-    row_y = lax.broadcasted_iota(jnp.int32, (PAD * 2 + by, LANES), 0) + (gy * by - PAD)
-    in_y = (row_y >= 0) & (row_y < ny * by)
-
-    fields = (f0, f1, f2, f3)
-    pieces = (p0, p1, p2)
-
-    def keep_pieces(m, row, column, value):
-        high, low = split_hi_lo(value)
-        pieces[m][row, column, :NRHS, :] = high
-        pieces[m][row, column, NRHS:, :] = low
-
-    def start_columns(x, columns, strength, row=None):
-        for j in columns:
-            tab = jnp.broadcast_to(tab_ext[x, pl.ds(j + PAD - S, 1), :], (NRHS, LANES))
-            value = lane_pick(gain, tab) * jnp.broadcast_to(strength(j + PAD - S), (NRHS, LANES))
-            f0[x, j] = value
-            if row is not None:
-                keep_pieces(0, row, j - S, value)
-            yield
-
-    def start_own(x, carry):
-        run(start_columns(x, range(S, S + by), lambda y: wide[2, x, pl.ds(y, 1), :], x - S))
-        return carry
-
-    def mask_row(x, sides):
-        row_x = gx * bx + x - S
-        inside = in_y & (row_x >= 0) & (row_x < nx * bx)
-        conduct[x] = jnp.where(inside, wide[0, x], 0.0)
-        charge[x] = jnp.where(inside, wide[2, x], 0.0)
-        for first, count in sides:
-            tab_ext[x, first : first + count, :] = wide[1, x, first : first + count, :].astype(jnp.int32)
-
-    def mask_own(x, carry):
-        mask_row(x, ((0, PAD), (PAD + by, PAD)))
-        sides = tuple(range(S)) + tuple(range(S + by, ey))
-        run(start_columns(x, sides, lambda y: charge[x, pl.ds(y, 1), :]))
-        return carry
-
-    def start_far(rows):
-        for x in rows:
-            mask_row(x, ((0, 2 * PAD + by),))
-        for x in rows:
-            yield from start_columns(x, range(ey), lambda y, x=x: charge[x, pl.ds(y, 1), :])
-
-    def weight_row(x, carry):
-        c = conduct[x]
-        zero = jnp.zeros_like(c)
-        rows = by + 2 * PAD
-        xm = c + conduct[x - 1]
-        xp = c + conduct[x + 1]
-        ym = c + pltpu.roll(c, 1, 0)
-        yp = c + pltpu.roll(c, rows - 1, 0)
-        low, top = lane > 0, lane < LANES - 1
-        zm = c + jnp.where(low, pltpu.roll(c, 1, 1), zero)
-        zp = c + jnp.where(top, pltpu.roll(c, LANES - 1, 1), zero)
-        total = ((xm + xp) + (ym + yp)) + (zm + zp)
-        inside = c > 0
-        inverse = jnp.where(inside, 1.0 / jnp.where(inside, total, 1.0), 0.0)
-        weight[0, x] = xm * inverse
-        weight[1, x] = xp * inverse
-        weight[2, x] = ym * inverse
-        weight[3, x] = yp * inverse
-        weight[4, x] = jnp.where(low, zm * inverse, zero)
-        weight[5, x] = jnp.where(top, zp * inverse, zero)
-        return carry
-
-    def mean_rows(src, x, count, columns, store):
-        before = [src[x + r, columns[0] - 1] for r in range(count)]
-        centre = [src[x + r, columns[0]] for r in range(count)]
-        for j in columns:
-            after = [src[x + r, j + 1] for r in range(count)]
-            edge = [src[x - 1, j]] + centre + [src[x + count, j]]
-            for r in range(count):
-                w = [jnp.broadcast_to(weight[d, x + r, pl.ds(j + PAD - S, 1), :], (NRHS, LANES)) for d in range(6)]
-                value = (w[0] * edge[r] + w[1] * edge[r + 2]) + (w[2] * before[r] + w[3] * after[r])
-                value = value + (w[4] * pltpu.roll(centre[r], 1, 1) + w[5] * pltpu.roll(centre[r], LANES - 1, 1))
-                store(r, j, value, centre[r])
-            before, centre = centre, after
-            yield
-
-    def inner_pair(m, x, rows):
-        def store(r, j, value, centre):
-            fields[m][x + r, j] = value
-            if m < S - 1 and rows[r] is not None and S <= j < S + by:
-                keep_pieces(m, rows[r], j - S, value)
-
-        return mean_rows(fields[m - 1], x, 2, range(m, ey - m), store)
-
-    def far_pair(m, first, i):
-        rows = []
-        for r in range(2):
-            spots = [first + 2 * k + r - S for k in range(2)]
-            inside = [0 <= spot < bx for spot in spots]
-            spots = [spot if ok else bx for spot, ok in zip(spots, inside)]
-            rows.append(spots[0] + (spots[1] - spots[0]) * i if any(inside) else None)
-        return inner_pair(m, first + 2 * i, rows)
-
-    def last_row(x):
-        row = x - S
-        step = 8
-        columns = []
-
-        def store(r, j, value, centre):
-            f4[row, j - S] = value
-            parts = [split_hi_lo(centre), split_hi_lo(value)]
-            highs = [p[row, j - S, :NRHS, :] for p in pieces] + [p[0] for p in parts]
-            lows = [p[row, j - S, NRHS:, :] for p in pieces] + [p[1] for p in parts]
-            columns.append(jnp.concatenate(highs + lows, axis=0))
-
-        for _ in mean_rows(f3, x, 1, range(S, S + by), store):
-            if len(columns) == step:
-                block = jnp.concatenate(columns, axis=1)
-                acc[...] += lax.dot_general(
-                    block[:ROWS], block, (((1,), (1,)), ((), ())), preferred_element_type=F32
-                )
-                columns.clear()
-            yield
-
-    def run(work):
-        for _ in work:
-            pass
-
-    def weave(work, count, other, extra):
-        done = 0
-        for k, _ in enumerate(work):
-            while done * count < extra * (k + 1):
-                next(other, None)
-                done += 1
-        run(other)
-
-    def rows_of(first, count, body):
-        lax.fori_loop(first, first + count, body, 0)
-
-    def pairs_of(m):
-        def body(i, carry):
-            x = S + m + 2 * i
-            run(inner_pair(m, x, (x - S, x + 1 - S)))
-            return carry
-
-        lax.fori_loop(0, bx // 2 - m, body, 0)
-
-    def twice(work):
-        def body(i, carry):
-            work(i)
-            return carry
-
-        lax.fori_loop(0, 2, body, 0)
-
-    def keep(m, first, count):
-        src = f4.at[pl.ds(first, count)] if m == S else fields[m].at[pl.ds(S + first, count), pl.ds(S, by)]
-        pltpu.make_async_copy(src, basis_hbm.at[m, pl.ds(first, count)], basis_sem).start()
-
-    rows_of(S, bx, start_own)
     keep(0, 0, bx)
+    rows_of(S + 1, bx - 2, weight_inner)
+    pairs_of(1, range(S + 1, S + by - 1))
     for copy in face_copies[2:4]:
         copy.wait_recv()
     rows_of(S, bx, mask_own)
-    rows_of(S + 1, bx - 2, weight_row)
-    for m in range(1, S):
-        pairs_of(m)
+    rows_of(S + 1, bx - 2, weight_sides)
+    pairs_of(1, range(1, S + 1), range(S + by - 1, ey - 1))
+    keep(1, 1, bx - 2)
+    for m in range(2, S):
+        pairs_of(m, None)
         keep(m, m, bx - 2 * m)
 
     for copy in face_copies[:2] + face_copies[4:]:
@@ -310,7 +325,7 @@
         run(last_row(x))
         return carry
 
-    rows_of(top, S, last_top)
+    lax.fori_loop(top, top + S, last_top, 0)
     keep(S, bx - S, S)
 
     both = acc[...]

time: 64 us -> 62.8 us (0.981)
  Pallas kernels: 63.1 us -> 61.9 us
    pallas_call x1, Pallas kernels: 51.4 us -> 50.2 us  [krylov_call(): pl.pallas_call(functools.partial(krylov_kernel, nx, ny), out_shape=(jax.S...]
where the time goes in v5:
time: 62.8 us; the launch traced here: 62.5 us
  Pallas kernels  61.9 us (99%)
  between operations  0.64 us (1%)
    pallas_call x1, Pallas kernels, krylov_call(): pl.pallas_call(functools.partial(krylov_kernel, nx, ny), out_shape=(jax.S...  50.2 us
    pallas_call x1, Pallas kernels, combine_call(): pl.pallas_call(combine_kernel, out_shape=(out, out), in_specs=[hbm, vmem]...  11.7 us

profile of v5, /device:TPU:1, one launch (start us, length us, event | category | flops | bytes accessed | tf_op | source)
XLA Modules:
  0.0 62.5 jit_solution(6845527037181526352)
XLA Ops:
  0.6 50.2 %shard_map.68 = (f32[5,16,32,16,128]{4,3,2,1,0:T(8,128)}, f32[32,128]{1,0:T(8,128)}) custom-call(s32[16,32,128]{2,1,0:T(8,128)} %phase_hbm.1, s32[16,32,128]{2,1,0:T(8,128)} %tab_hbm.1, f32[16,32,128]{2,1,0:T(8,128)} %source_hbm.1, f32[3]{0:T(128)} %sigma_ref.1, f32[16,64]{1,0:T(8,128)} %gain_ref.1), custom_call_target="tpu_custom_call" | custom-call | tf_op jit(solution)/shard_map/pallas_call | solution.py:459
  50.9 11.7 %shard_map.69 = (f32[16,16,32,128]{3,2,1,0:T(8,128)}, f32[16,16,32,128]{3,2,1,0:T(8,128)}) custom-call(f32[5,16,32,16,128]{4,3,2,1,0:T(8,128)} %get-tuple-element.4.basis_hbm, f32[32,128]{1,0:T(8,128)} %get-tuple-element.5.total_ref), custom_call_target="tpu_custom_call" | custom-call | tf_op jit(solution)/shard_map/pallas_call | solution.py:504

commit v6 on v5

--- a/solution.py
+++ b/solution.py
@@ -38,8 +38,8 @@
     )
 
 
-def krylov_kernel(nx, ny, phase_hbm, tab_hbm, source_hbm, sigma_ref, gain_ref, basis_hbm, total_ref,
-                  phase_own, tab_ext, wide, conduct, charge, weight, f0, f1, f2, f3, f4, p0, p1, p2, acc,
+def krylov_kernel(nx, ny, phase_hbm, tab_hbm, source_hbm, sigma_hbm, gain_hbm, basis_hbm, total_ref,
+                  sigma_ref, gain_ref, phase_own, tab_ext, wide, conduct, charge, weight, f0, f1, f2, f3, f4, p0, p1, p2, acc,
                   part1, part2, part3, own_sem, face_send, face_recv, basis_sem, ring_send, ring_recv):
     bx, by = phase_hbm.shape[0], phase_hbm.shape[1]
     ex = bx + 2 * S
@@ -64,6 +64,8 @@
         pltpu.make_async_copy(phase_hbm, phase_own, own_sem.at[0]),
         pltpu.make_async_copy(tab_hbm, tab_ext.at[own], own_sem.at[1]),
         pltpu.make_async_copy(source_hbm, wide.at[(2,) + own], own_sem.at[2]),
+        pltpu.make_async_copy(sigma_hbm, sigma_ref, own_sem.at[3]),
+        pltpu.make_async_copy(gain_hbm, gain_ref, own_sem.at[4]),
     ]
     for copy in own_copies:
         copy.start()
@@ -79,10 +81,10 @@
             for y in (0, PAD + by):
                 wide[a, x, y : y + PAD, :] = corner
     acc[...] = jnp.zeros_like(acc)
+    for copy in own_copies:
+        copy.wait()
     sigma0, sigma1, sigma2 = sigma_ref[0], sigma_ref[1], sigma_ref[2]
     gain = jnp.concatenate([gain_ref[...], jnp.zeros((NRHS, LANES - gain_ref.shape[1]), F32)], axis=1)
-    for copy in own_copies:
-        copy.wait()
 
     def fill_row(r, carry):
         phase = phase_own[r]
@@ -114,8 +116,43 @@
                 keep_pieces(0, row, j - S, value)
             yield
 
+    tabs = gain_ref.shape[1]
+    rest = gain_ref[...]
+    gain_parts = []
+    for _ in range(3):
+        gain_parts.append(rest.astype(BF16))
+        rest = rest - gain_parts[-1].astype(F32)
+    gain_stack = jnp.concatenate(gain_parts, axis=0)
+    tab_row = lax.broadcasted_iota(jnp.int32, (tabs, LANES), 0)
+
+    def start_pairs(x, columns, strength, row=None):
+        for k in range(0, len(columns), 2):
+            pair = columns[k : k + 2]
+            picks = []
+            for j in pair:
+                tab = jnp.broadcast_to(tab_ext[x, pl.ds(j + PAD - S, 1), :], (tabs, LANES))
+                picks.append(jnp.where(tab == tab_row, 1.0, 0.0).astype(BF16))
+            parts = jnp.dot(gain_stack, jnp.concatenate(picks, axis=1), preferred_element_type=F32)
+            picked = parts[:NRHS] + (parts[NRHS : 2 * NRHS] + parts[2 * NRHS :])
+            for n, j in enumerate(pair):
+                value = picked[:, n * LANES : (n + 1) * LANES]
+                value = value * jnp.broadcast_to(strength(j + PAD - S), (NRHS, LANES))
+                f0[x, j] = value
+                if row is not None:
+                    keep_pieces(0, row, j - S, value)
+            yield
+
     def start_own(x, carry):
-        run(start_columns(x, range(S, S + by), lambda y: wide[2, x, pl.ds(y, 1), :], x - S))
+        def strength(y):
+            return wide[2, x, pl.ds(y, 1), :]
+
+        split = S + 16
+        weave(
+            start_columns(x, range(S, split), strength, x - S),
+            16,
+            start_pairs(x, range(split, S + by), strength, x - S),
+            (by - 16) // 2,
+        )
         return carry
 
     def mask_row(x, sides):
@@ -130,8 +167,13 @@
 
     def mask_own(x, carry):
         mask_row(x, ((0, PAD), (PAD + by, PAD)))
-        sides = tuple(range(S)) + tuple(range(S + by, ey))
-        run(start_columns(x, sides, lambda y: charge[x, pl.ds(y, 1), :]))
+
+        def strength(y):
+            return charge[x, pl.ds(y, 1), :]
+
+        weave(
+            start_columns(x, range(S), strength), S, start_pairs(x, range(S + by, ey), strength), S // 2
+        )
         return carry
 
     def start_far(rows):
@@ -218,7 +260,7 @@
             if len(columns) == step:
                 block = jnp.concatenate(columns, axis=1)
                 acc[...] += lax.dot_general(
-                    block[:ROWS], block, (((1,), (1,)), ((), ())), preferred_element_type=F32
+                    block, block[:ROWS], (((1,), (1,)), ((), ())), preferred_element_type=F32
                 )
                 columns.clear()
             yield
@@ -330,12 +372,9 @@
 
     both = acc[...]
     lane_g = lax.broadcasted_iota(jnp.int32, (ROWS, LANES), 1)
-    first = both[:, :LANES]
-    second = jnp.concatenate([both[:, LANES:], jnp.zeros((ROWS, 2 * LANES - 2 * ROWS), F32)], axis=1)
-    cross = pltpu.roll(jnp.where(lane_g >= ROWS, first, second), LANES - ROWS, 1)
-    cross = jnp.where(lane_g < ROWS, cross, 0.0)
+    cross = jnp.concatenate([both[ROWS:], jnp.zeros((ROWS, LANES - ROWS), F32)], axis=1)
     square = jnp.concatenate([cross, jnp.zeros((LANES - ROWS, LANES), F32)], axis=0)
-    gram = jnp.where(lane_g < ROWS, first, 0.0) + cross + square.T[:ROWS]
+    gram = jnp.concatenate([both[:ROWS], jnp.zeros((ROWS, LANES - ROWS), F32)], axis=1) + cross + square.T[:ROWS]
     lane_b = lane_g[:NRHS]
     blocks = [gram[m * NRHS : (m + 1) * NRHS] for m in range(S + 1)]
     part1[gy, :NRHS] = blocks[0] + jnp.where(lane_b < ROWS, 0.0, pltpu.roll(blocks[2], 48, 1))
@@ -462,9 +501,11 @@
             jax.ShapeDtypeStruct((S + 1, bx, by, NRHS, LANES), F32),
             jax.ShapeDtypeStruct(packed, F32),
         ),
-        in_specs=[hbm, hbm, hbm, pl.BlockSpec(memory_space=pltpu.SMEM), vmem],
+        in_specs=[hbm] * 5,
         out_specs=(hbm, vmem),
         scratch_shapes=[
+            pltpu.SMEM(sigma_table.shape, F32),
+            pltpu.VMEM(gain.shape, F32),
             pltpu.VMEM((bx, by, LANES), jnp.int32),
             pltpu.VMEM(wide, jnp.int32),
             pltpu.VMEM((3,) + wide, F32),
@@ -478,11 +519,11 @@
             pltpu.VMEM((bx + 1, by, 2 * NRHS, LANES), BF16),
             pltpu.VMEM((bx + 1, by, 2 * NRHS, LANES), BF16),
             pltpu.VMEM((bx + 1, by, 2 * NRHS, LANES), BF16),
-            pltpu.VMEM((ROWS, 2 * ROWS), F32),
+            pltpu.VMEM((2 * ROWS, ROWS), F32),
             pltpu.VMEM((ny,) + packed, F32),
             pltpu.VMEM((RING_X,) + packed, F32),
             pltpu.VMEM((ring_z,) + packed, F32),
-            dma((3,)),
+            dma((5,)),
             dma((8,)),
             dma((8,)),
             dma(()),

time: 62.8 us -> 60.5 us (0.963)
  Pallas kernels: 61.9 us -> 59.7 us
    pallas_call x1, Pallas kernels: 50.2 us -> 48 us  [krylov_call(): pl.pallas_call(functools.partial(krylov_kernel, nx, ny), out_shape=(jax.S...]
where the time goes in v6:
time: 60.5 us; the launch traced here: 60.3 us
  Pallas kernels  59.7 us (99%)
  between operations  0.64 us (1%)
    pallas_call x1, Pallas kernels, krylov_call(): pl.pallas_call(functools.partial(krylov_kernel, nx, ny), out_shape=(jax.S...  48 us
    pallas_call x1, Pallas kernels, combine_call(): pl.pallas_call(combine_kernel, out_shape=(out, out), in_specs=[hbm, vmem]...  11.7 us

profile of v6, /device:TPU:1, one launch (start us, length us, event | category | flops | bytes accessed | tf_op | source)
XLA Modules:
  0.0 60.3 jit_solution(15671689004310634275)
XLA Ops:
  0.6 48.0 %shard_map.68 = (f32[5,16,32,16,128]{4,3,2,1,0:T(8,128)}, f32[32,128]{1,0:T(8,128)}) custom-call(s32[16,32,128]{2,1,0:T(8,128)} %phase_hbm.1, s32[16,32,128]{2,1,0:T(8,128)} %tab_hbm.1, f32[16,32,128]{2,1,0:T(8,128)} %source_hbm.1, f32[3]{0:T(128)} %sigma_hbm.1, f32[16,64]{1,0:T(8,128)} %gain_hbm.1), custom_call_target="tpu_custom_call" | custom-call | tf_op jit(solution)/shard_map/pallas_call | solution.py:498
  48.7 11.7 %shard_map.69 = (f32[16,16,32,128]{3,2,1,0:T(8,128)}, f32[16,16,32,128]{3,2,1,0:T(8,128)}) custom-call(f32[5,16,32,16,128]{4,3,2,1,0:T(8,128)} %get-tuple-element.4.basis_hbm, f32[32,128]{1,0:T(8,128)} %get-tuple-element.5.total_ref), custom_call_target="tpu_custom_call" | custom-call | tf_op jit(solution)/shard_map/pallas_call | solution.py:545

commit v7 on v6

--- a/solution.py
+++ b/solution.py
@@ -277,17 +277,17 @@
                 done += 1
         run(other)
 
-    def rows_of(first, count, body):
-        lax.fori_loop(first, first + count, body, 0, unroll=2)
-
-    def pairs_of(m, *parts):
+    def rows_of(first, count, body, unroll=2):
+        lax.fori_loop(first, first + count, body, 0, unroll=unroll)
+
+    def pairs_of(m, *parts, unroll=1):
         def body(i, carry):
             x = S + m + 2 * i
             for columns in parts:
                 run(inner_pair(m, x, (x - S, x + 1 - S), columns))
             return carry
 
-        lax.fori_loop(0, bx // 2 - m, body, 0)
+        lax.fori_loop(0, bx // 2 - m, body, 0, unroll=unroll)
 
     def twice(work):
         def body(i, carry):
@@ -300,7 +300,7 @@
         src = f4.at[pl.ds(first, count)] if m == S else fields[m].at[pl.ds(S + first, count), pl.ds(S, by)]
         pltpu.make_async_copy(src, basis_hbm.at[m, pl.ds(first, count)], basis_sem).start()
 
-    rows_of(S, bx, start_own)
+    rows_of(S, bx, start_own, 4)
     pl.semaphore_wait(barrier, len(peers))
 
     x_all, y_all = (0, bx), (0, by)
@@ -330,16 +330,16 @@
         copy.start()
         face_copies.append(copy)
     keep(0, 0, bx)
-    rows_of(S + 1, bx - 2, weight_inner)
+    rows_of(S + 1, bx - 2, weight_inner, 7)
     pairs_of(1, range(S + 1, S + by - 1))
     for copy in face_copies[2:4]:
         copy.wait_recv()
-    rows_of(S, bx, mask_own)
-    rows_of(S + 1, bx - 2, weight_sides)
-    pairs_of(1, range(1, S + 1), range(S + by - 1, ey - 1))
+    rows_of(S, bx, mask_own, 4)
+    rows_of(S + 1, bx - 2, weight_sides, 7)
+    pairs_of(1, range(1, S + 1), range(S + by - 1, ey - 1), unroll=7)
     keep(1, 1, bx - 2)
     for m in range(2, S):
-        pairs_of(m, None)
+        pairs_of(m, None, unroll=3 if m == 2 else 1)
         keep(m, m, bx - 2 * m)
 
     for copy in face_copies[:2] + face_copies[4:]:
@@ -347,13 +347,13 @@
     low, top, inner = S, bx, 2 * S
     wide_pair = 2 * ey
     twice(lambda i: weave(last_row(inner + i), by, start_far((2 * i, 2 * i + 1)), wide_pair))
-    rows_of(1, S, weight_row)
+    rows_of(1, S, weight_row, S)
     twice(lambda i: weave(last_row(inner + 2 + i), by, far_pair(1, 1, i), ey - 2))
     twice(lambda i: weave(last_row(inner + 4 + i), by, far_pair(2, 2, i), ey - 4))
     far = S + bx
     twice(lambda i: weave(last_row(inner + 6 + i), by, start_far((far + 2 * i, far + 2 * i + 1)), wide_pair))
     keep(S, S, bx - 2 * S)
-    rows_of(far - 1, S, weight_row)
+    rows_of(far - 1, S, weight_row, S)
     twice(lambda i: run(far_pair(3, 3, i)))
     twice(lambda i: weave(last_row(low + i), by, far_pair(1, far - 1, i), ey - 2))
     twice(lambda i: weave(last_row(low + 2 + i), by, far_pair(2, far - 2, i), ey - 4))
@@ -552,7 +552,7 @@
             pltpu.VMEM((bx, NRHS, by + PAD, LANES), F32),
             pltpu.VMEM((bx, NRHS, by + PAD, LANES), F32),
             pltpu.VMEM((4 * NRHS, 2 * LANES), BF16),
-            dma((bx // 2,)),
+            dma((bx // 4,)),
             dma(()),
             dma(()),
         ],

time: 60.5 us -> 57.9 us (0.957)
  Pallas kernels: 59.7 us -> 56.8 us
    pallas_call x1, Pallas kernels: 48 us -> 45.8 us  [krylov_call(): pl.pallas_call(functools.partial(krylov_kernel, nx, ny), out_shape=(jax.S...]
where the time goes in v7:
time: 57.9 us; the launch traced here: 57.5 us
  Pallas kernels  56.8 us (98%)
  between operations  0.64 us (1%)
    pallas_call x1, Pallas kernels, krylov_call(): pl.pallas_call(functools.partial(krylov_kernel, nx, ny), out_shape=(jax.S...  45.8 us
    pallas_call x1, Pallas kernels, combine_call(): pl.pallas_call(combine_kernel, out_shape=(out, out), in_specs=[hbm, vmem]...  11.1 us

profile of v7, /device:TPU:1, one launch (start us, length us, event | category | flops | bytes accessed | tf_op | source)
XLA Modules:
  0.0 57.5 jit_solution(18152759596963486883)
XLA Ops:
  0.6 45.8 %shard_map.68 = (f32[5,16,32,16,128]{4,3,2,1,0:T(8,128)}, f32[32,128]{1,0:T(8,128)}) custom-call(s32[16,32,128]{2,1,0:T(8,128)} %phase_hbm.1, s32[16,32,128]{2,1,0:T(8,128)} %tab_hbm.1, f32[16,32,128]{2,1,0:T(8,128)} %source_hbm.1, f32[3]{0:T(128)} %sigma_hbm.1, f32[16,64]{1,0:T(8,128)} %gain_hbm.1), custom_call_target="tpu_custom_call" | custom-call | tf_op jit(solution)/shard_map/pallas_call | solution.py:498
  46.4 11.1 %shard_map.69 = (f32[16,16,32,128]{3,2,1,0:T(8,128)}, f32[16,16,32,128]{3,2,1,0:T(8,128)}) custom-call(f32[5,16,32,16,128]{4,3,2,1,0:T(8,128)} %get-tuple-element.4.basis_hbm, f32[32,128]{1,0:T(8,128)} %get-tuple-element.5.total_ref), custom_call_target="tpu_custom_call" | custom-call | tf_op jit(solution)/shard_map/pallas_call | solution.py:545

commit v8 on v7

--- a/solution.py
+++ b/solution.py
@@ -289,12 +289,12 @@
 
         lax.fori_loop(0, bx // 2 - m, body, 0, unroll=unroll)
 
-    def twice(work):
+    def twice(work, unroll=1):
         def body(i, carry):
             work(i)
             return carry
 
-        lax.fori_loop(0, 2, body, 0)
+        lax.fori_loop(0, 2, body, 0, unroll=unroll)
 
     def keep(m, first, count):
         src = f4.at[pl.ds(first, count)] if m == S else fields[m].at[pl.ds(S + first, count), pl.ds(S, by)]
@@ -339,7 +339,7 @@
     pairs_of(1, range(1, S + 1), range(S + by - 1, ey - 1), unroll=7)
     keep(1, 1, bx - 2)
     for m in range(2, S):
-        pairs_of(m, None, unroll=3 if m == 2 else 1)
+        pairs_of(m, None, unroll=3 if m == 2 else 5)
         keep(m, m, bx - 2 * m)
 
     for copy in face_copies[:2] + face_copies[4:]:
@@ -354,11 +354,11 @@
     twice(lambda i: weave(last_row(inner + 6 + i), by, start_far((far + 2 * i, far + 2 * i + 1)), wide_pair))
     keep(S, S, bx - 2 * S)
     rows_of(far - 1, S, weight_row, S)
-    twice(lambda i: run(far_pair(3, 3, i)))
+    twice(lambda i: run(far_pair(3, 3, i)), 2)
     twice(lambda i: weave(last_row(low + i), by, far_pair(1, far - 1, i), ey - 2))
     twice(lambda i: weave(last_row(low + 2 + i), by, far_pair(2, far - 2, i), ey - 4))
     keep(S, 0, S)
-    twice(lambda i: run(far_pair(3, far - 3, i)))
+    twice(lambda i: run(far_pair(3, far - 3, i)), 2)
     for m in range(1, S):
         keep(m, 0, m)
         keep(m, bx - m, m)
@@ -367,7 +367,7 @@
         run(last_row(x))
         return carry
 
-    lax.fori_loop(top, top + S, last_top, 0)
+    lax.fori_loop(top, top + S, last_top, 0, unroll=2)
     keep(S, bx - S, S)
 
     both = acc[...]

time: 57.9 us -> 57.2 us (0.988)
  Pallas kernels: 56.8 us -> 56 us
    pallas_call x1, Pallas kernels: 45.8 us -> 44.9 us  [krylov_call(): pl.pallas_call(functools.partial(krylov_kernel, nx, ny), out_shape=(jax.S...]
where the time goes in v8:
time: 57.2 us; the launch traced here: 56.8 us
  Pallas kernels  56 us (98%)
  between operations  0.8 us (1%)
    pallas_call x1, Pallas kernels, krylov_call(): pl.pallas_call(functools.partial(krylov_kernel, nx, ny), out_shape=(jax.S...  44.9 us
    pallas_call x1, Pallas kernels, combine_call(): pl.pallas_call(combine_kernel, out_shape=(out, out), in_specs=[hbm, vmem]...  11.1 us

profile of v8, /device:TPU:1, one launch (start us, length us, event | category | flops | bytes accessed | tf_op | source)
XLA Modules:
  0.0 56.8 jit_solution(1367763023462302638)
XLA Ops:
  0.6 44.9 %shard_map.68 = (f32[5,16,32,16,128]{4,3,2,1,0:T(8,128)}, f32[32,128]{1,0:T(8,128)}) custom-call(s32[16,32,128]{2,1,0:T(8,128)} %phase_hbm.1, s32[16,32,128]{2,1,0:T(8,128)} %tab_hbm.1, f32[16,32,128]{2,1,0:T(8,128)} %source_hbm.1, f32[3]{0:T(128)} %sigma_hbm.1, f32[16,64]{1,0:T(8,128)} %gain_hbm.1), custom_call_target="tpu_custom_call" | custom-call | tf_op jit(solution)/shard_map/pallas_call | solution.py:498
  45.6 11.1 %shard_map.69 = (f32[16,16,32,128]{3,2,1,0:T(8,128)}, f32[16,16,32,128]{3,2,1,0:T(8,128)}) custom-call(f32[5,16,32,16,128]{4,3,2,1,0:T(8,128)} %get-tuple-element.4.basis_hbm, f32[32,128]{1,0:T(8,128)} %get-tuple-element.5.total_ref), custom_call_target="tpu_custom_call" | custom-call | tf_op jit(solution)/shard_map/pallas_call | solution.py:545
